TPU v7x, 128 devices: a whole 4x4x4 slice. The times are simulated.
128 devices in a mesh: section: 2 (over core), shard: 2 (over z_hi), replica: 32 (over y, z_lo, x).
Axes of the slice: x: 4, y: 4, z: 4 (z_hi: 2, z_lo: 2; z = z_hi * 2 + z_lo), core: 2. Of those that a mesh axis runs over, the one named last changes fastest.
Arguments:
- layer_input: bfloat16 [128, 128, 1152], P('replica'), may hold values from -6 to 6
- cotangent: bfloat16 [128, 128, 1152], P('replica'), may hold values from -6 to 6
- attn_gain: float32 [2, 1152], P('section'), may hold values from 0.5 to 1.5
- query_weight: bfloat16 [2, 1152, 1152], P('section', None, 'shard'), may hold values from -0.1875 to 0.1875
- key_matrix: bfloat16 [2, 1152, 384], P('section', None, 'shard'), may hold values from -0.1875 to 0.1875
- value_matrix: bfloat16 [2, 1152, 384], P('section', None, 'shard'), may hold values from -0.1875 to 0.1875
- output_weight: bfloat16 [2, 1152, 1152], P('section', 'shard'), may hold values from -0.75 to 0.75
- ffn_gain: float32 [2, 1152], P('section'), may hold values from 0.5 to 1.5
- gate_weight: bfloat16 [2, 1152, 3072], P('section', None, 'shard'), may hold values from -0.1875 to 0.1875
- up_weight: bfloat16 [2, 1152, 3072], P('section', None, 'shard'), may hold values from -0.1875 to 0.1875
- down_weight: bfloat16 [2, 3072, 1152], P('section', 'shard'), may hold values from -0.109375 to 0.109375
Outputs:
- activations: bfloat16 [2, 128, 128, 1152], P('section', 'replica')
- input_grads: bfloat16 [2, 128, 128, 1152], P('section', 'replica')
- attn_gain_grad: float32 [2, 1152], P('section', 'replica')
- query_grad: float32 [2, 1152, 1152], P('section', 'replica', 'shard')
- key_grad: float32 [2, 1152, 384], P('section', 'replica', 'shard')
- value_grad: float32 [2, 1152, 384], P('section', 'replica', 'shard')
- output_grad: float32 [2, 1152, 1152], P('section', 'shard', 'replica')
- ffn_gain_grad: float32 [2, 1152], P('section', 'replica')
- gate_grad: float32 [2, 1152, 3072], P('section', 'replica', 'shard')
- up_grad: float32 [2, 1152, 3072], P('section', 'replica', 'shard')
- down_grad: float32 [2, 3072, 1152], P('section', 'shard', 'replica')
All inputs are finite; a program needn't handle non-finite values.
Results may differ from a plain program's by a relative error of at most 0.03.
Values may be sent and summed in bfloat16 or wider, within the bound.
A program may use at most 256 MiB of HBM per device.

v0:
```python
import jax
import jax.numpy as jnp
from jax import lax
from jax.sharding import PartitionSpec as P

QUERY_HEADS = 18
KEY_VALUE_HEADS = 6
HEAD_SIZE = 64


EPSILON = 1e-05
ROPE_BASE = 10000.0


def passed_along(value, axis, steps):
    count = lax.axis_size(axis)
    leading, last = (max(0, -steps), min(count, count - steps))
    return lax.ppermute(value, axis, [(source, source + steps) for source in range(leading, last)])


def rope_tables(sequence_length, head_size):
    half_size = head_size // 2
    position = jnp.arange(sequence_length, dtype=jnp.float32)
    frequency = ROPE_BASE ** (-jnp.arange(half_size, dtype=jnp.float32) * 2.0 / head_size)
    angles = position[:, None] * frequency[None, :]
    return (jnp.cos(angles), jnp.sin(angles))


def rotary_apply(heads, cosine_lookup, sine_lookup):
    half_size = heads.shape[-1] // 2
    first_half = heads[..., :half_size]
    second_half = heads[..., half_size:]
    cosine_part = cosine_lookup[:, None, :]
    sine_part = sine_lookup[:, None, :]
    return jnp.concatenate(
        [
            first_half * cosine_part - second_half * sine_part,
            second_half * cosine_part + first_half * sine_part,
        ],
        -1,
    )


def rotate_back(heads, cosine_lookup, sine_lookup):
    half_size = heads.shape[-1] // 2
    first_half = heads[..., :half_size]
    second_half = heads[..., half_size:]
    cosine_part = cosine_lookup[:, None, :]
    sine_part = sine_lookup[:, None, :]
    return jnp.concatenate(
        [
            first_half * cosine_part + second_half * sine_part,
            second_half * cosine_part - first_half * sine_part,
        ],
        -1,
    )


def norm_scale(value_rows):
    return lax.rsqrt(jnp.mean(value_rows * value_rows, axis=-1, keepdims=True) + EPSILON)


def norm_back(value_rows, norm_factor, grad_rows):
    return norm_factor * grad_rows - value_rows * norm_factor**3 * jnp.mean(
        grad_rows * value_rows, axis=-1, keepdims=True
    )


def dense(left, right, form):
    return jnp.einsum(form, left, right, preferred_element_type=jnp.float32)


def masked_scores(grouped_heads, key_head_rows):
    sequence_length = grouped_heads.shape[0]
    raw_scores = dense(grouped_heads, key_head_rows, "lkgd,mkd->kglm") * HEAD_SIZE ** (-0.5)
    causal = jnp.arange(sequence_length)[:, None] >= jnp.arange(sequence_length)[None, :]
    return jnp.where(causal, raw_scores, -1e30)


def forward_layer(hidden_in, params, cosine_lookup, sine_lookup):
    (
        gain_attn,
        weight_q,
        key_weight_param,
        value_weight_param,
        weight_o,
        gain_ffn,
        weight_gate,
        weight_up,
        weight_down,
    ) = params
    sequence_length = hidden_in.shape[0]
    local_kv = key_weight_param.shape[1] // HEAD_SIZE
    group_count = QUERY_HEADS // KEY_VALUE_HEADS
    normalized_rows = (hidden_in * norm_scale(hidden_in) * gain_attn).astype(jnp.bfloat16)
    query_rows = rotary_apply(
        dense(normalized_rows, weight_q, "ld,dq->lq").reshape(
            sequence_length, local_kv * group_count, HEAD_SIZE
        ),
        cosine_lookup,
        sine_lookup,
    ).astype(jnp.bfloat16)
    key_head_rows = rotary_apply(
        dense(normalized_rows, key_weight_param, "ld,dq->lq").reshape(
            sequence_length, local_kv, HEAD_SIZE
        ),
        cosine_lookup,
        sine_lookup,
    ).astype(jnp.bfloat16)
    value_rows = (
        dense(normalized_rows, value_weight_param, "ld,dq->lq")
        .astype(jnp.bfloat16)
        .reshape(sequence_length, local_kv, HEAD_SIZE)
    )
    grouped_heads = query_rows.reshape(sequence_length, local_kv, group_count, HEAD_SIZE)
    scores = masked_scores(grouped_heads, key_head_rows)
    row_top = jnp.max(scores, axis=-1, keepdims=True)
    exponent = jnp.exp(scores - row_top)
    row_total = jnp.sum(exponent, axis=-1, keepdims=True)
    probabilities = exponent / row_total
    log_total = row_top + jnp.log(row_total)
    mixed_heads = (
        dense(probabilities.astype(jnp.bfloat16), value_rows, "kglm,mkd->lkgd")
        .astype(jnp.bfloat16)
        .reshape(sequence_length, local_kv * group_count * HEAD_SIZE)
    )
    attended = lax.psum(dense(mixed_heads, weight_o, "lq,qd->ld"), "shard")
    middle = hidden_in + attended
    ffn_in = (middle * norm_scale(middle) * gain_ffn).astype(jnp.bfloat16)
    gate_pre = dense(ffn_in, weight_gate, "ld,df->lf")
    up_pre = dense(ffn_in, weight_up, "ld,df->lf")
    hidden = (jax.nn.silu(gate_pre) * up_pre).astype(jnp.bfloat16)
    result = middle + lax.psum(
        dense(hidden, weight_down, "lf,fd->ld").astype(jnp.bfloat16), "shard"
    ).astype(jnp.float32)
    kept_state = (
        hidden_in,
        normalized_rows,
        query_rows,
        key_head_rows,
        value_rows,
        log_total,
        mixed_heads,
        middle,
        ffn_in,
        gate_pre,
        up_pre,
        hidden,
    )
    return (result, kept_state)


def backward_ffn(out_grad, kept_state, params):
    (
        hidden_in,
        normalized_rows,
        query_rows,
        key_head_rows,
        value_rows,
        log_total,
        mixed_heads,
        middle,
        ffn_in,
        gate_pre,
        up_pre,
        hidden,
    ) = kept_state
    gain_ffn, weight_gate, weight_up, weight_down = params[5:]
    down_in = out_grad.astype(jnp.bfloat16)
    down_term = dense(hidden, down_in, "lf,ld->fd")
    hidden_grad = dense(down_in, weight_down, "ld,fd->lf")
    sigmoid_gate = jax.nn.sigmoid(gate_pre)
    swish_gate = gate_pre * sigmoid_gate
    gate_back = (
        hidden_grad * up_pre * sigmoid_gate * (1.0 + gate_pre * (1.0 - sigmoid_gate))
    ).astype(jnp.bfloat16)
    up_back = (hidden_grad * swish_gate).astype(jnp.bfloat16)
    gate_term = dense(ffn_in, gate_back, "ld,lf->df")
    up_term = dense(ffn_in, up_back, "ld,lf->df")
    partial_rows = dense(gate_back, weight_gate, "lf,df->ld") + dense(
        up_back, weight_up, "lf,df->ld"
    )
    ffn_in_back = lax.psum(partial_rows.astype(jnp.bfloat16), "shard").astype(jnp.float32)
    norm_factor = norm_scale(middle)
    gain_term = jnp.sum(ffn_in_back * middle * norm_factor, axis=0)
    middle_back = out_grad + norm_back(middle, norm_factor, ffn_in_back * gain_ffn)
    return (middle_back, (gain_term, gate_term, up_term, down_term))


def backward_attn(middle_back, kept_state, params, cosine_lookup, sine_lookup):
    (
        hidden_in,
        normalized_rows,
        query_rows,
        key_head_rows,
        value_rows,
        log_total,
        mixed_heads,
        middle,
        ffn_in,
        gate_pre,
        up_pre,
        hidden,
    ) = kept_state
    gain_attn, weight_q, key_weight_param, value_weight_param, weight_o = params[:5]
    sequence_length = middle_back.shape[0]
    local_kv = key_head_rows.shape[1]
    group_count = QUERY_HEADS // KEY_VALUE_HEADS
    attn_in = middle_back.astype(jnp.bfloat16)
    out_term = dense(mixed_heads, attn_in, "lq,ld->qd")
    mixed_back = (
        dense(attn_in, weight_o, "ld,qd->lq")
        .astype(jnp.bfloat16)
        .reshape(sequence_length, local_kv, group_count, HEAD_SIZE)
    )
    grouped_heads = query_rows.reshape(sequence_length, local_kv, group_count, HEAD_SIZE)
    probabilities = jnp.exp(masked_scores(grouped_heads, key_head_rows) - log_total)
    value_back = dense(probabilities.astype(jnp.bfloat16), mixed_back, "kglm,lkgd->mkd")
    prob_back = dense(mixed_back, value_rows, "lkgd,mkd->kglm")
    score_back = (
        probabilities * (prob_back - jnp.sum(prob_back * probabilities, axis=-1, keepdims=True))
    ).astype(jnp.bfloat16)
    query_turned = dense(score_back, key_head_rows, "kglm,mkd->lkgd") * HEAD_SIZE ** (-0.5)
    key_turned = dense(score_back, grouped_heads, "kglm,lkgd->mkd") * HEAD_SIZE ** (-0.5)
    query_back = (
        rotate_back(
            query_turned.reshape(sequence_length, local_kv * group_count, HEAD_SIZE),
            cosine_lookup,
            sine_lookup,
        )
        .reshape(sequence_length, local_kv * group_count * HEAD_SIZE)
        .astype(jnp.bfloat16)
    )
    key_back = (
        rotate_back(key_turned, cosine_lookup, sine_lookup)
        .reshape(sequence_length, local_kv * HEAD_SIZE)
        .astype(jnp.bfloat16)
    )
    value_low = value_back.reshape(sequence_length, local_kv * HEAD_SIZE).astype(jnp.bfloat16)
    query_term = dense(normalized_rows, query_back, "ld,lq->dq")
    key_term = dense(normalized_rows, key_back, "ld,lq->dq")
    value_term = dense(normalized_rows, value_low, "ld,lq->dq")
    partial_rows = (
        dense(query_back, weight_q, "lq,dq->ld")
        + dense(key_back, key_weight_param, "lq,dq->ld")
        + dense(value_low, value_weight_param, "lq,dq->ld")
    )
    normed_back = lax.psum(partial_rows.astype(jnp.bfloat16), "shard").astype(jnp.float32)
    norm_factor = norm_scale(hidden_in)
    gain_term = jnp.sum(normed_back * hidden_in * norm_factor, axis=0)
    input_grad = middle_back + norm_back(hidden_in, norm_factor, normed_back * gain_attn)
    return (input_grad, (gain_term, query_term, key_term, value_term, out_term))


def on_device(
    layer_input,
    cotangent,
    attn_gain,
    query_weight,
    key_matrix,
    value_matrix,
    output_weight,
    ffn_gain,
    gate_weight,
    up_weight,
    down_weight,
):
    section_index = lax.axis_index("section")
    first_section = section_index == 0
    micro_count = layer_input.shape[0]
    sequence_length = layer_input.shape[1]
    params = tuple(
        (
            item_array[0]
            for item_array in (
                attn_gain,
                query_weight,
                key_matrix,
                value_matrix,
                output_weight,
                ffn_gain,
                gate_weight,
                up_weight,
                down_weight,
            )
        )
    )
    cosine_lookup, sine_lookup = rope_tables(sequence_length, HEAD_SIZE)
    received = jnp.zeros(layer_input.shape[1:], jnp.bfloat16)
    outputs_local = jnp.zeros(layer_input.shape, jnp.bfloat16)
    kept_list = []
    for tick_index in range(micro_count + 1):
        micro_index = tick_index - section_index
        valid_tick = (micro_index >= 0) & (micro_index < micro_count)
        clamped = jnp.clip(micro_index, 0, micro_count - 1)
        fresh_rows = lax.dynamic_index_in_dim(layer_input, clamped, 0, keepdims=False)
        arriving = jnp.where(first_section, fresh_rows, received)
        result, kept_state = forward_layer(
            arriving.astype(jnp.float32), params, cosine_lookup, sine_lookup
        )
        result_low = result.astype(jnp.bfloat16)
        outputs_local = jnp.where(
            valid_tick,
            lax.dynamic_update_index_in_dim(outputs_local, result_low, clamped, 0),
            outputs_local,
        )
        kept_list.append(kept_state)
        if tick_index < micro_count:
            received = passed_along(result_low, "section", 1)
    stacked = jax.tree.map(lambda *arrays: jnp.stack(arrays), *kept_list)
    attn_sums = tuple((jnp.zeros(item_array.shape, jnp.float32) for item_array in params[:5]))
    ffn_sums = tuple((jnp.zeros(item_array.shape, jnp.float32) for item_array in params[5:]))
    grads_local = jnp.zeros(layer_input.shape, jnp.bfloat16)
    back_received = jnp.zeros(layer_input.shape[1:], jnp.bfloat16)
    for tick_index in range(micro_count + 1):
        micro_index = tick_index - 1 + section_index
        valid_tick = (micro_index >= 0) & (micro_index < micro_count)
        clamped = jnp.clip(micro_index, 0, micro_count - 1)
        source_tick = jnp.clip(micro_index + section_index, 0, micro_count)
        kept_state = jax.tree.map(
            lambda item_array: lax.dynamic_index_in_dim(item_array, source_tick, 0, keepdims=False),
            stacked,
        )
        given_rows = lax.dynamic_index_in_dim(cotangent, clamped, 0, keepdims=False)
        arriving = jnp.where(first_section, back_received, given_rows).astype(jnp.float32)
        middle_back, ffn_terms = backward_ffn(arriving, kept_state, params)
        ffn_sums = tuple(
            (
                jnp.where(valid_tick, running + term, running)
                for running, term in zip(ffn_sums, ffn_terms)
            )
        )
        input_grad, attn_terms = backward_attn(
            middle_back, kept_state, params, cosine_lookup, sine_lookup
        )
        attn_sums = tuple(
            (
                jnp.where(valid_tick, running + term, running)
                for running, term in zip(attn_sums, attn_terms)
            )
        )
        grad_low = input_grad.astype(jnp.bfloat16)
        grads_local = jnp.where(
            valid_tick,
            lax.dynamic_update_index_in_dim(grads_local, grad_low, clamped, 0),
            grads_local,
        )
        if tick_index < micro_count:
            back_received = passed_along(grad_low, "section", -1)
    all_done = tuple(
        (
            lax.psum_scatter(
                attn_sums[0][None].astype(jnp.bfloat16), "replica", scatter_dimension=1, tiled=True
            ).astype(jnp.float32),
            lax.psum_scatter(
                attn_sums[1][None].astype(jnp.bfloat16), "replica", scatter_dimension=1, tiled=True
            ).astype(jnp.float32),
            lax.psum_scatter(
                attn_sums[2][None].astype(jnp.bfloat16), "replica", scatter_dimension=1, tiled=True
            ).astype(jnp.float32),
            lax.psum_scatter(
                attn_sums[3][None].astype(jnp.bfloat16), "replica", scatter_dimension=1, tiled=True
            ).astype(jnp.float32),
            lax.psum_scatter(
                attn_sums[4][None].astype(jnp.bfloat16), "replica", scatter_dimension=2, tiled=True
            ).astype(jnp.float32),
            lax.psum_scatter(
                ffn_sums[0][None].astype(jnp.bfloat16), "replica", scatter_dimension=1, tiled=True
            ).astype(jnp.float32),
            lax.psum_scatter(
                ffn_sums[1][None].astype(jnp.bfloat16), "replica", scatter_dimension=1, tiled=True
            ).astype(jnp.float32),
            lax.psum_scatter(
                ffn_sums[2][None].astype(jnp.bfloat16), "replica", scatter_dimension=1, tiled=True
            ).astype(jnp.float32),
            lax.psum_scatter(
                ffn_sums[3][None].astype(jnp.bfloat16), "replica", scatter_dimension=2, tiled=True
            ).astype(jnp.float32),
        )
    )
    return (outputs_local[None], grads_local[None]) + all_done


def solution(mesh):
    in_specs = (
        P("replica", None, None),
        P("replica", None, None),
        P("section", None),
        P("section", None, "shard"),
        P("section", None, "shard"),
        P("section", None, "shard"),
        P("section", "shard", None),
        P("section", None),
        P("section", None, "shard"),
        P("section", None, "shard"),
        P("section", "shard", None),
    )
    out_specs = (
        P("section", "replica", None, None),
        P("section", "replica", None, None),
        P("section", "replica"),
        P("section", "replica", "shard"),
        P("section", "replica", "shard"),
        P("section", "replica", "shard"),
        P("section", "shard", "replica"),
        P("section", "replica"),
        P("section", "replica", "shard"),
        P("section", "replica", "shard"),
        P("section", "shard", "replica"),
    )
    return jax.shard_map(
        on_device, mesh=mesh, in_specs=in_specs, out_specs=out_specs, check_vma=False
    )
```

profile of v0, /device:TPU:0, one launch (start us, length us, event | category | flops | bytes accessed | tf_op | source)
XLA Modules:
  0.0 1403.4 jit_solution(3263321741603485869)
XLA Ops:
  32.7 29.6 %all-reduce.36.cloned.1.call-done = f32[128,1152]{1,0:T(8,128)} async-done(((f32[128,1152]{1,0:T(8,128)}), f32[128,1152]{1,0:T(8,128)}) %all-reduce.36.cloned.1.call-update) | async-done | bytes 589840 | tf_op jit(solution)/shard_map/psum | solution.py:127
  65.8 3.6 bitcast_dynamic-update-slice_fusion.4
  75.5 28.8 %all-reduce.38.cloned.1.call-done = bf16[128,1152]{1,0:T(8,128)(2,1)} async-done(((bf16[128,1152]{1,0:T(8,128)(2,1)}), bf16[128,1152]{1,0:T(8,128)(2,1)}) %all-reduce.38.cloned.1.call-update) | async-done | bytes 294928 | tf_op jit(solution)/shard_map/psum | solution.py:133
  122.3 30.2 %all-reduce.40.cloned.1.call-done = f32[128,1152]{1,0:T(8,128)} async-done(((f32[128,1152]{1,0:T(8,128)}), f32[128,1152]{1,0:T(8,128)}) %all-reduce.40.cloned.1.call-update) | async-done | bytes 589840 | tf_op jit(solution)/shard_map/psum | solution.py:127
  156.0 3.6 bitcast_dynamic-update-slice_fusion.3
  165.6 29.1 %all-reduce.42.cloned.1.call-done = bf16[128,1152]{1,0:T(8,128)(2,1)} async-done(((bf16[128,1152]{1,0:T(8,128)(2,1)}), bf16[128,1152]{1,0:T(8,128)(2,1)}) %all-reduce.42.cloned.1.call-update) | async-done | bytes 294928 | tf_op jit(solution)/shard_map/psum | solution.py:133
  214.5 30.2 %all-reduce.44.cloned.1.call-done = f32[128,1152]{1,0:T(8,128)} async-done(((f32[128,1152]{1,0:T(8,128)}), f32[128,1152]{1,0:T(8,128)}) %all-reduce.44.cloned.1.call-update) | async-done | bytes 589840 | tf_op jit(solution)/shard_map/psum | solution.py:127
  248.2 3.6 bitcast_dynamic-update-slice_fusion.2
  257.7 29.1 %all-reduce.46.cloned.1.call-done = bf16[128,1152]{1,0:T(8,128)(2,1)} async-done(((bf16[128,1152]{1,0:T(8,128)(2,1)}), bf16[128,1152]{1,0:T(8,128)(2,1)}) %all-reduce.46.cloned.1.call-update) | async-done | bytes 294928 | tf_op jit(solution)/shard_map/psum | solution.py:133
  306.2 30.2 %all-reduce.48.cloned.1.call-done = f32[128,1152]{1,0:T(8,128)} async-done(((f32[128,1152]{1,0:T(8,128)}), f32[128,1152]{1,0:T(8,128)}) %all-reduce.48.cloned.1.call-update) | async-done | bytes 589840 | tf_op jit(solution)/shard_map/psum | solution.py:127
  339.9 3.6 bitcast_dynamic-update-slice_fusion.1
  349.5 29.1 %all-reduce.50.cloned.1.call-done = bf16[128,1152]{1,0:T(8,128)(2,1)} async-done(((bf16[128,1152]{1,0:T(8,128)(2,1)}), bf16[128,1152]{1,0:T(8,128)(2,1)}) %all-reduce.50.cloned.1.call-update) | async-done | bytes 294928 | tf_op jit(solution)/shard_map/psum | solution.py:133
  409.8 23.6 %all-reduce.52.cloned.1.call-done = f32[128,1152]{1,0:T(8,128)} async-done(((f32[128,1152]{1,0:T(8,128)}), f32[128,1152]{1,0:T(8,128)}) %all-reduce.52.cloned.1.call-update) | async-done | bytes 589840 | tf_op jit(solution)/shard_map/psum | solution.py:127
  450.9 5.0 convolution_select_fusion.1
  455.9 4.9 convolution_select_fusion.2
  464.2 5.1 convolution_select_fusion
  469.4 24.6 %all-reduce.54.cloned.1.call-done = bf16[128,1152]{1,0:T(8,128)(2,1)} async-done(((bf16[128,1152]{1,0:T(8,128)(2,1)}), bf16[128,1152]{1,0:T(8,128)(2,1)}) %all-reduce.54.cloned.1.call-update) | async-done | bytes 294928 | tf_op jit(solution)/shard_map/psum | solution.py:183
  510.7 3.1 convolution_select_fusion.4
  513.8 28.0 %all-reduce.56.cloned.1.call-done = bf16[128,1152]{1,0:T(8,128)(2,1)} async-done(((bf16[128,1152]{1,0:T(8,128)(2,1)}), bf16[128,1152]{1,0:T(8,128)(2,1)}) %all-reduce.56.cloned.1.call-update) | async-done | bytes 294928 | tf_op jit(solution)/shard_map/psum | solution.py:248
  541.8 2.8 fusion.329
  553.5 2.8 fusion.256
  561.1 7.3 add_select_fusion.11
  568.5 7.3 add_select_fusion.7
  575.7 5.1 add_select_fusion.3
  580.8 11.0 all-reduce.58.cloned.1.call-done
  599.4 3.0 fusion.444
  604.1 4.1 add_select_fusion.15
  608.2 2.9 add_select_fusion.19
  611.1 24.0 %all-reduce.60.cloned.1.call-done = bf16[128,1152]{1,0:T(8,128)(2,1)} async-done(((bf16[128,1152]{1,0:T(8,128)(2,1)}), bf16[128,1152]{1,0:T(8,128)(2,1)}) %all-reduce.60.cloned.1.call-update) | async-done | bytes 294928 | tf_op jit(solution)/shard_map/psum | solution.py:248
  646.5 2.8 fusion.247
  653.9 7.2 add_select_fusion.10
  661.2 7.2 add_select_fusion.6
  668.4 17.2 %all-reduce.62.cloned.1.call-done = bf16[128,1152]{1,0:T(8,128)(2,1)} async-done(((bf16[128,1152]{1,0:T(8,128)(2,1)}), bf16[128,1152]{1,0:T(8,128)(2,1)}) %all-reduce.62.cloned.1.call-update) | async-done | bytes 294928 | tf_op jit(solution)/shard_map/psum | solution.py:183
  695.1 4.1 add_select_fusion.14
  699.2 2.9 add_select_fusion.18
  702.2 24.0 %all-reduce.64.cloned.1.call-done = bf16[128,1152]{1,0:T(8,128)(2,1)} async-done(((bf16[128,1152]{1,0:T(8,128)(2,1)}), bf16[128,1152]{1,0:T(8,128)(2,1)}) %all-reduce.64.cloned.1.call-update) | async-done | bytes 294928 | tf_op jit(solution)/shard_map/psum | solution.py:248
  745.0 7.2 add_select_fusion.9
  752.2 7.3 add_select_fusion.5
  759.5 5.0 fusion.407
  764.6 12.1 all-reduce.66.cloned.1.call-done
  786.2 4.1 add_select_fusion.13
  790.3 2.9 add_select_fusion.17
  793.2 24.0 %all-reduce.68.cloned.1.call-done = bf16[128,1152]{1,0:T(8,128)(2,1)} async-done(((bf16[128,1152]{1,0:T(8,128)(2,1)}), bf16[128,1152]{1,0:T(8,128)(2,1)}) %all-reduce.68.cloned.1.call-update) | async-done | bytes 294928 | tf_op jit(solution)/shard_map/psum | solution.py:248
  828.6 2.8 fusion.229
  831.5 5.3 fusion.405
  841.1 10.9 fusion.5
  852.0 16.5 %copy.73 = bf16[1,1536,1152]{1,0,2:T(2,128)(2,1)} copy(bf16[1,1536,1152]{2,1,0:T(8,128)(2,1)} %fusion.5) | data formatting | bytes 7077888 | tf_op jit(solution)/shard_map/convert_element_type | solution.py:377
  868.5 6.2 fusion.7
  886.4 3.7 copy.71
  892.5 3.7 copy.70
  896.2 3.5 fusion.70
  899.7 6.8 copy.72
  906.6 3.5 fusion.71
  910.1 6.8 copy.69
  916.9 6.4 fusion.6
  923.4 172.3 %fusion.671 = (bf16[40,1536]{1,0:T(8,128)(2,1)}, bf16[40,1536]{1,0:T(8,128)(2,1)}) fusion(bf16[1,1152,1536]{2,1,0:T(8,128)(2,1)} %fusion.7, bf16[1,1152,1536]{2,1,0:T(8,128)(2,1)} %fusion.6), kind=kCustom, calls=%all-reduce-scatter.2 | all-reduce-scatter fusion | flops 3932161 | bytes 7324160
  1102.2 3.0 collective-permute-start.11
  1109.5 6.4 collective-permute-start.14
  1117.8 4.9 collective-permute-start.12
  1122.6 13.6 collective-permute-start.15
  1136.3 7.9 concatenate.305
  1146.0 7.9 concatenate.306
  1159.8 123.1 %all-reduce.11 = (bf16[1,1152]{1,0:T(2,128)(2,1)}, bf16[1,1152]{1,0:T(2,128)(2,1)}) all-reduce(bf16[1,1152]{1,0:T(2,128)(2,1)S(1)} %fusion.645, bf16[1,1152]{1,0:T(2,128)(2,1)} %fusion.646), channel_id=2, replica_groups=mesh['section'=2,'shard'=2,'replica'=32] {'replica'}, use_global_device_ids=true, to_apply=%region_70.71.clone | all-reduce | flops 2304 | bytes 9216
  1290.6 97.6 %all-reduce.72.cloned.1.call-done = (bf16[1,1152,576]{2,0,1:T(2,128)(2,1)}, bf16[1,1152,192]{2,0,1:T(2,128)(2,1)}, bf16[1,1152,192]{2,0,1:T(2,128)(2,1)}, bf16[1...) async-done(((bf16[1,1152,576]{2,0,1:T(2,128)(2,1)}, bf16[1,1152,192]{2,0,1:T(2,128)(2,1)}, bf16[1,1152,192]{2,0,1:T(2,128)(2,1)}, bf16[1,576,1152]{1,0,2:T(2,128)(2,1)}, ...) | async-done | bytes 7077904
  (763 shorter events, 328.2 us)
Async XLA Ops:
  7.2 62.2 %copy-start = (bf16[1,1152,1536]{2,1,0:T(8,128)(2,1)S(1)}, bf16[1,1152,1536]{2,1,0:T(8,128)(2,1)}, u32[]{:S(2)}) copy-start(bf16[1,1152,1536]{2,1,0:T(8,128)(2,1)} %param.20) | copy-start | bytes 10616836
  7.2 55.0 %all-reduce.36.cloned.1.call-start = ((), (), s32[]{:S(2)}) async-start(), calls=%async_computation | async-start | bytes 1179648 | tf_op jit(solution)/shard_map/psum | solution.py:127
  21.4 82.9 %all-reduce.38.cloned.1.call-start = ((), (), s32[]{:S(2)}) async-start(), calls=%async_computation.1 | async-start | bytes 589824 | tf_op jit(solution)/shard_map/psum | solution.py:133
  73.2 79.3 %all-reduce.40.cloned.1.call-start = ((), (), s32[]{:S(2)}) async-start(), calls=%async_computation.2 | async-start | bytes 1179648 | tf_op jit(solution)/shard_map/psum | solution.py:127
  106.0 2.7 collective-permute-start
  115.0 79.7 %all-reduce.42.cloned.1.call-start = ((), (), s32[]{:S(2)}) async-start(), calls=%async_computation.3 | async-start | bytes 589824 | tf_op jit(solution)/shard_map/psum | solution.py:133
  163.5 81.2 %all-reduce.44.cloned.1.call-start = ((), (), s32[]{:S(2)}) async-start(), calls=%async_computation.4 | async-start | bytes 1179648 | tf_op jit(solution)/shard_map/psum | solution.py:127
  194.7 8.3 copy-start.48
  194.7 8.3 copy-start.88
  194.7 8.7 copy-start.39
  196.9 4.0 collective-permute-start.1
  207.2 79.6 %all-reduce.46.cloned.1.call-start = ((), (), s32[]{:S(2)}) async-start(), calls=%async_computation.5 | async-start | bytes 589824 | tf_op jit(solution)/shard_map/psum | solution.py:133
  255.7 80.7 %all-reduce.48.cloned.1.call-start = ((), (), s32[]{:S(2)}) async-start(), calls=%async_computation.6 | async-start | bytes 1179648 | tf_op jit(solution)/shard_map/psum | solution.py:127
  286.8 7.8 copy-start.49
  286.8 7.8 copy-start.89
  286.8 8.2 copy-start.40
  289.1 3.5 collective-permute-start.2
  298.9 79.7 %all-reduce.50.cloned.1.call-start = ((), (), s32[]{:S(2)}) async-start(), calls=%async_computation.7 | async-start | bytes 589824 | tf_op jit(solution)/shard_map/psum | solution.py:133
  347.5 86.0 %all-reduce.52.cloned.1.call-start = ((), (), s32[]{:S(2)}) async-start(), calls=%async_computation.8 | async-start | bytes 1179648 | tf_op jit(solution)/shard_map/psum | solution.py:127
  380.8 6.0 collective-permute-start.3
  395.9 98.1 %all-reduce.54.cloned.1.call-start = ((), (), s32[]{:S(2)}) async-start(), calls=%async_computation.9 | async-start | bytes 589824 | tf_op jit(solution)/shard_map/psum | solution.py:183
  395.9 9.4 copy-start.167
  395.9 10.0 copy-start.130
  396.0 9.9 copy-start.187
  396.0 9.9 copy-start.189
  396.0 11.9 copy-start.127
  396.0 11.8 copy-start.188
  433.4 7.4 copy-start.1
  462.8 78.9 %all-reduce.56.cloned.1.call-start = ((), (), s32[]{:S(2)}) async-start(), calls=%async_computation.10 | async-start | bytes 589824 | tf_op jit(solution)/shard_map/psum | solution.py:248
  510.6 81.2 %all-reduce.58.cloned.1.call-start = ((), (), s32[]{:S(2)}) async-start(), calls=%async_computation.11 | async-start | bytes 589824 | tf_op jit(solution)/shard_map/psum | solution.py:183
  544.6 8.9 copy-start.30
  549.0 3.5 collective-permute-start.4
  560.6 74.5 %all-reduce.60.cloned.1.call-start = ((), (), s32[]{:S(2)}) async-start(), calls=%async_computation.12 | async-start | bytes 589824 | tf_op jit(solution)/shard_map/psum | solution.py:248
  561.1 7.4 copy-start.103
  561.1 14.6 %slice-start = ((s8[7077888]{0:T(1024)(128)(4,1)}), s8[4194304]{0:T(1024)(128)(4,1)S(1)}, s32[]{:S(2)}) async-start(s8[7077888]{0:T(1024)(128)(4,1)} %bitcast.1343), calls=%async_computation.20 | async-start | bytes 8388608
  568.5 7.3 copy-start.98
  604.0 81.6 %all-reduce.62.cloned.1.call-start = ((), (), s32[]{:S(2)}) async-start(), calls=%async_computation.13 | async-start | bytes 589824 | tf_op jit(solution)/shard_map/psum | solution.py:183
  635.2 8.2 copy-start.81
  635.2 8.2 copy-start.143
  639.6 5.9 collective-permute-start.5
  653.7 72.5 %all-reduce.64.cloned.1.call-start = ((), (), s32[]{:S(2)}) async-start(), calls=%async_computation.14 | async-start | bytes 589824 | tf_op jit(solution)/shard_map/psum | solution.py:248
  695.0 81.6 %all-reduce.66.cloned.1.call-start = ((), (), s32[]{:S(2)}) async-start(), calls=%async_computation.15 | async-start | bytes 589824 | tf_op jit(solution)/shard_map/psum | solution.py:183
  726.2 8.2 copy-start.86
  726.2 8.2 copy-start.147
  730.7 5.9 collective-permute-start.6
  744.7 72.5 %all-reduce.68.cloned.1.call-start = ((), (), s32[]{:S(2)}) async-start(), calls=%async_computation.16 | async-start | bytes 589824 | tf_op jit(solution)/shard_map/psum | solution.py:248
  752.2 7.3 copy-start.95
  786.1 88.5 %all-reduce.70.cloned.1.call-start = ((), (), s32[]{:S(2)}) async-start(), calls=%async_computation.17 | async-start | bytes 589824 | tf_op jit(solution)/shard_map/psum | solution.py:183
  817.3 8.2 copy-start.83
  817.3 8.2 copy-start.145
  821.7 5.9 collective-permute-start.7
  840.8 316.3 %all-reduce.74.cloned.1.call-start = ((), (), s32[]{:S(2)}) async-start(), calls=%async_computation.19 | async-start | bytes 1179648 | tf_op jit(solution)/shard_map/psum | solution.py:133
  890.1 498.1 %all-reduce.72.cloned.1.call-start = ((), (), s32[]{:S(2)}) async-start(), calls=%async_computation.18 | async-start | bytes 30670848
  923.4 181.8 %copy-start.196 = (f32[128]{0:T(128)S(1)}, f32[128]{0:T(128)}, u32[]{:S(2)}) copy-start(f32[128]{0:T(128)} %get-tuple-element.57) | copy-start | bytes 1540
  1096.4 21.4 %collective-permute-start.10 = (bf16[40,1536]{1,0:T(8,128)(2,1)}, bf16[40,1536]{1,0:T(8,128)(2,1)}, u32[]{:S(2)}, u32[]{:S(2)}) collective-permute-start(bf16[40,1536]{1,0:T(8,128)(2,1)} %get-tuple-element.72), channel_id=1, source_target_pairs={{0,3},{1,4},{2,5},{3,6},{4,7},{5,8},{6,9},{7,10},{8,11},{9,12},{10... | collective-permute-start | bytes 368648
  1098.3 24.3 %collective-permute-start.9 = (bf16[40,1536]{1,0:T(8,128)(2,1)}, bf16[40,1536]{1,0:T(8,128)(2,1)}, u32[]{:S(2)}, u32[]{:S(2)}) collective-permute-start(bf16[40,1536]{1,0:T(8,128)(2,1)} %get-tuple-element.72), channel_id=1, source_target_pairs={{0,2},{1,3},{2,4},{3,5},{4,6},{5,7},{6,8},{7,9},{8,10},{9,11},{10,... | collective-permute-start | bytes 368648
  1100.3 36.0 %collective-permute-start.8 = (bf16[40,1536]{1,0:T(8,128)(2,1)}, bf16[40,1536]{1,0:T(8,128)(2,1)}, u32[]{:S(2)}, u32[]{:S(2)}) collective-permute-start(bf16[40,1536]{1,0:T(8,128)(2,1)} %get-tuple-element.72), channel_id=1, source_target_pairs={{0,1},{1,2},{2,3},{3,4},{4,5},{5,6},{6,7},{7,8},{8,9},{9,10},{10,1... | collective-permute-start | bytes 368648
  1102.2 13.6 collective-permute-start.11
  1105.7 50.0 %copy-start.173 = (f32[1152]{0:T(1024)S(1)}, f32[1152]{0:T(1024)}, u32[]{:S(2)}) copy-start(f32[1152]{0:T(1024)} %get-tuple-element.35) | copy-start | bytes 13828
  1105.7 51.4 %copy-start.92 = (f32[1152]{0:T(1024)S(1)}, f32[1152]{0:T(1024)}, u32[]{:S(2)}) copy-start(f32[1152]{0:T(1024)} %reduce) | copy-start | bytes 13828
  1109.5 36.5 %collective-permute-start.14 = (bf16[40,1536]{1,0:T(8,128)(2,1)}, bf16[40,1536]{1,0:T(8,128)(2,1)}, u32[]{:S(2)}, u32[]{:S(2)}) collective-permute-start(bf16[40,1536]{1,0:T(8,128)(2,1)} %get-tuple-element.73), channel_id=1, source_target_pairs={{0,3},{1,4},{2,5},{3,6},{4,7},{5,8},{6,9},{7,10},{8,11},{9,12},{10... | collective-permute-start | bytes 368648
  1115.8 30.2 %collective-permute-start.13 = (bf16[40,1536]{1,0:T(8,128)(2,1)}, bf16[40,1536]{1,0:T(8,128)(2,1)}, u32[]{:S(2)}, u32[]{:S(2)}) collective-permute-start(bf16[40,1536]{1,0:T(8,128)(2,1)} %get-tuple-element.73), channel_id=1, source_target_pairs={{0,2},{1,3},{2,4},{3,5},{4,6},{5,7},{6,8},{7,9},{8,10},{9,11},{10,... | collective-permute-start | bytes 368648
  1117.8 28.2 %collective-permute-start.12 = (bf16[40,1536]{1,0:T(8,128)(2,1)}, bf16[40,1536]{1,0:T(8,128)(2,1)}, u32[]{:S(2)}, u32[]{:S(2)}) collective-permute-start(bf16[40,1536]{1,0:T(8,128)(2,1)} %get-tuple-element.73), channel_id=1, source_target_pairs={{0,1},{1,2},{2,3},{3,4},{4,5},{5,6},{6,7},{7,8},{8,9},{9,10},{10,1... | collective-permute-start | bytes 368648
  1122.6 23.4 %collective-permute-start.15 = (bf16[4,1536]{1,0:T(4,128)(2,1)}, bf16[4,1536]{1,0:T(4,128)(2,1)}, u32[]{:S(2)}, u32[]{:S(2)}) collective-permute-start(bf16[4,1536]{1,0:T(4,128)(2,1)} %slice.201), channel_id=1, source_target_pairs={{0,4},{1,5},{2,6},{3,7},{4,8},{5,9},{6,10},{7,11},{8,12},{9,13},{1... | collective-permute-start | bytes 36872
  (173 other events, 507.6 us)
Sparse Core Ops, SparseCore 0:
  21.6 40.6 all-reduce.35
  73.3 30.9 all-reduce.37
  115.1 37.3 all-reduce.39
  163.6 30.9 all-reduce.41
  207.3 37.3 all-reduce.43
  255.8 30.9 all-reduce.45
  299.0 37.3 all-reduce.47
  347.6 30.9 all-reduce.49
  396.0 37.3 all-reduce.51
  462.9 30.9 all-reduce.53
  510.7 30.9 all-reduce.55
  560.8 30.9 all-reduce.57
  604.1 30.9 all-reduce.59
  653.8 31.7 all-reduce.61
  695.2 30.9 all-reduce.63
  744.8 31.7 all-reduce.65
  786.2 30.9 all-reduce.67
  841.0 31.7 all-reduce.69
  890.2 38.2 all-reduce.73
  931.3 456.8 all-reduce.71
where the time goes:
time: 1420 us; the launch traced here: 1400 us
  waiting for transfers between devices  524 us (37%)
  blocking collectives  295 us (21%)
  matrix products  270 us (19%)
  other arithmetic  144 us (10%)
  local copies, waits for them, and re-layouts  102 us (7%)
  starting transfers between devices  49.9 us (4%)
  between operations  18.9 us (1%)
    unnamed x2, blocking collectives  295 us
    dot_general x140, matrix products, dense(): return jnp.einsum(form, left, right, preferred_element_type=jnp.float32)  270 us
    psum x5, waiting for transfers between devices, forward_layer(): attended = lax.psum(dense(mixed_heads, weight_o, 'lq,qd->ld'), 'shard')  144 us
    psum x5, waiting for transfers between devices, forward_layer(): lax.psum(dense(hidden, weight_down, 'lf,fd->ld').astype(jnp.bfloat16), 's...  116 us
    psum x4, waiting for transfers between devices, backward_attn(): lax.psum(partial_rows.astype(jnp.bfloat16), 'shard').astype(jnp.float32)  100 us
    unnamed x29, waiting for transfers between devices  97.9 us
    psum x5, waiting for transfers between devices, backward_ffn(): lax.psum(partial_rows.astype(jnp.bfloat16), 'shard').astype(jnp.float32)  64.8 us
    unnamed x423, local copies, waits for them, and re-layouts  58.4 us
  transfers between devices with their start and end apart: 36, of which 20 were waited for; matrix products, arithmetic and copies ran while one was open for 31% of the time, Pallas kernels for 0%

commit v1 on v0

v1 whole, which is shorter than its diff:
```python
import functools

import jax
import jax.numpy as jnp
import numpy as np
from jax import lax
from jax.experimental import pallas as pl
from jax.experimental.pallas import tpu as pltpu
from jax.sharding import PartitionSpec as P

HEAD = 64
HEADS = 9
GROUPS = 3
WIDTH = 1152
FF = 1536
LEN = 128
SEQS = 4
TOKENS = LEN * SEQS
QW = HEADS * HEAD
KW = GROUPS * HEAD
RING = 4
PIECE = 80
ROWS = RING * RING * PIECE
OWN = WIDTH // 32
EPSILON = 1e-05
ROPE_BASE = 10000.0
F32 = jnp.float32
BF16 = jnp.bfloat16
MESH = pl.DeviceIdType.MESH
PART_DOWN, PART_GATE, PART_UP, PART_MIX = 0, 1, 2, 3
PARTS = ((1536, "x"), (1536, "y"), (1536, "y"), (1664, "x"))
BLOCKS = (
    (0, 0, 768, 384),
    (1, 0, 768, 384),
    (0, 768, 768, 384),
    (1, 768, 768, 384),
    (3, 0, 768, 384),
    (2, 0, 768, 384),
    (3, 768, 896, 512),
    (2, 768, 768, 384),
)


def dot(left, right):
    return lax.dot_general(left, right, (((1,), (0,)), ((), ())), preferred_element_type=F32)


def dot_nt(left, right):
    return lax.dot_general(left, right, (((1,), (1,)), ((), ())), preferred_element_type=F32)


def dot_tn(left, right):
    return lax.dot_general(left, right, (((0,), (0,)), ((), ())), preferred_element_type=F32)


def rope_tables():
    half = HEAD // 2
    position = np.arange(LEN, dtype=np.float32)
    frequency = (ROPE_BASE ** (-np.arange(half, dtype=np.float32) * 2.0 / HEAD)).astype(np.float32)
    angles = position[:, None] * frequency[None, :]
    cosine = np.cos(angles).astype(np.float32)
    sine = np.sin(angles).astype(np.float32)
    return (
        np.tile(np.concatenate([cosine, cosine], 1), (1, HEADS)),
        np.tile(np.concatenate([sine, sine], 1), (1, HEADS)),
    )


def turn_matrix():
    turn = np.zeros((QW, QW), np.float32)
    for head in range(HEADS):
        for j in range(HEAD // 2):
            first, second = head * HEAD + j, head * HEAD + HEAD // 2 + j
            turn[second, first] = -1.0
            turn[first, second] = 1.0
    return turn


def place_matrix():
    place = np.zeros((RING, RING, PIECE, WIDTH), np.float32)
    for y in range(RING):
        for x in range(RING):
            for z in range(2):
                owner = (y * 2 + z) * RING + x
                for i in range(OWN):
                    place[y, x, z * 40 + i, owner * OWN + i] = 1.0
    return place.reshape(ROWS, WIDTH)


def rms_factor(rows):
    return lax.rsqrt(jnp.mean(rows * rows, axis=-1, keepdims=True) + EPSILON)


def norm_back(rows, factor, grad):
    return factor * grad - rows * factor**3 * jnp.mean(grad * rows, axis=-1, keepdims=True)


def sequence(m):
    return pl.ds(pl.multiple_of(m * LEN, LEN), LEN)


def compute_kernel(
    x_ref, cot_ref, ga_ref, wq_ref, wk_ref, wv_ref, wo_ref, gf_ref, wg_ref, wu_ref, wd_ref,
    cos_ref, sin_ref, turn_ref, place_ref,
    act_ref, ig_ref, g0_ref, g1_ref, g2_ref, g3_ref,
    wqr, wkr, hin, gin, normed, qs, qr, ks, kr, vs, probs, mixed, middle, ffn_in, gates, ups, hidden,
    attn_in, qkv_back, gain_acc, xt, snd, rcv, act_stage, ig_stage, g_stage,
    in_sem, in_send, hin_sem, gin_sem, ar_send, ar_recv, step_send, out_sem, out_send, g_sem,
):
    section = lax.axis_index("section")
    shard = lax.axis_index("shard")
    rep = lax.axis_index("replica")
    zlo = lax.rem(lax.div(rep, RING), 2)
    side = rep + RING - 2 * RING * zlo
    core = {"section": 1 - section}
    twin = {"shard": 1 - shard, "replica": side}
    swap = {"replica": side}

    barrier = pltpu.get_barrier_semaphore()
    for target in (core, twin, swap):
        pl.semaphore_signal(barrier, inc=1, device_id=target, device_id_type=MESH)
    pl.semaphore_wait(barrier, 3)

    def fetch(source, target, sem, m):
        rows = sequence(m)

        def local():
            return pltpu.make_async_copy(source.at[m], target.at[rows], sem.at[m])

        def push():
            return pltpu.make_async_remote_copy(
                source.at[m], target.at[rows], in_send.at[m], sem.at[m],
                device_id=swap, device_id_type=MESH,
            )

        return local, push

    for m in range(SEQS):
        for s, (source, target, sem) in enumerate(((x_ref, hin, hin_sem), (cot_ref, gin, gin_sem))):
            local, push = fetch(source, target, sem, m)

            @pl.when((section == s) & (shard == 0))
            def _():
                local().start()

            @pl.when((section == s) & (shard == 1))
            def _():
                push().start()

    def wait_rows(source, target, sem, m, s):
        local, push = fetch(source, target, sem, m)

        @pl.when((section == s) & (shard == 0))
        def _():
            local().wait()

        @pl.when((section == s) & (shard == 1))
        def _():
            push().wait_recv()

    def pass_on(stage, target, sem, m, which):
        rows = sequence(m)
        return pltpu.make_async_remote_copy(
            stage.at[rows], target.at[rows], step_send.at[which, m], sem.at[m],
            device_id=core, device_id_type=MESH,
        )

    def exchange(phase, m):
        rows = sequence(m)
        return pltpu.make_async_remote_copy(
            snd.at[phase, rows], rcv.at[phase, rows], ar_send.at[phase, m], ar_recv.at[phase, m],
            device_id=twin, device_id_type=MESH,
        )

    def exchanged(phase, m):
        exchange(phase, m).wait_recv()
        rows = sequence(m)
        return snd[phase, rows, :].astype(F32) + rcv[phase, rows, :].astype(F32)

    def emit(stage, target, which, m):
        rows = sequence(m)

        def local():
            return pltpu.make_async_copy(stage.at[rows], target.at[m], out_sem.at[which, m])

        def push():
            return pltpu.make_async_remote_copy(
                stage.at[rows], target.at[m], out_send.at[which, m], out_sem.at[which, m],
                device_id=swap, device_id_type=MESH,
            )

        return local, push

    def start_emit(stage, target, which, m):
        local, push = emit(stage, target, which, m)

        @pl.when(shard == 0)
        def _():
            local().start()

        @pl.when(shard == 1)
        def _():
            push().start()

    turn = turn_ref[...]
    wqr[...] = dot(wq_ref[...], turn).astype(BF16)
    wkr[...] = dot(wk_ref[...], turn[:KW, :KW]).astype(BF16)
    gain_acc[...] = jnp.zeros_like(gain_acc)
    mixed[:, QW:] = jnp.zeros((TOKENS, 64), BF16)
    qkv_back[:, QW + 2 * KW:] = jnp.zeros((TOKENS, 64), BF16)

    def stacked(value, g):
        return jnp.concatenate(
            [value[:, (3 * g + j) * HEAD:(3 * g + j + 1) * HEAD] for j in range(3)], axis=0
        )

    def attention(m):
        rows = sequence(m)
        wait_rows(x_ref, hin, hin_sem, m, 0)

        @pl.when(section == 1)
        def _():
            pass_on(act_stage, hin, hin_sem, m, 0).wait_recv()

        h = hin[rows, :].astype(F32)
        normal = (h * rms_factor(h) * ga_ref[...]).astype(BF16)
        normed[rows, :] = normal
        cosine, sine = cos_ref[...], sin_ref[...]
        query = (dot(normal, wq_ref[...]) * cosine + dot(normal, wqr[...]) * sine).astype(BF16)
        key = (
            dot(normal, wk_ref[...]) * cosine[:, :KW] + dot(normal, wkr[...]) * sine[:, :KW]
        ).astype(BF16)
        value = dot(normal, wv_ref[...]).astype(BF16)
        qs[rows, :] = query
        ks[rows, :] = key
        vs[rows, :] = value
        qr[rows, :] = dot(query, turn_ref[...]).astype(BF16)
        kr[rows, :] = dot(key, turn_ref[:KW, :KW]).astype(BF16)
        at = lax.rem(lax.broadcasted_iota(jnp.int32, (3 * LEN, LEN), 0), LEN)
        causal = at >= lax.broadcasted_iota(jnp.int32, (3 * LEN, LEN), 1)
        heads = []
        for g in range(GROUPS):
            cols = slice(g * HEAD, (g + 1) * HEAD)
            scores = dot_nt(stacked(query, g), key[:, cols]) * HEAD**-0.5
            scores = jnp.where(causal, scores, -1e30)
            top = jnp.max(scores, axis=-1, keepdims=True)
            weight = jnp.exp(scores - top)
            prob = (weight / jnp.sum(weight, axis=-1, keepdims=True)).astype(BF16)
            probs[m, g] = prob
            out = dot(prob, value[:, cols]).astype(BF16)
            heads += [out[j * LEN:(j + 1) * LEN] for j in range(3)]
        mix = jnp.concatenate(heads, axis=1)
        mixed[rows, :QW] = mix
        snd[0, rows, :] = dot(mix, wo_ref[...]).astype(BF16)
        exchange(0, m).start()

    def feed_forward(m):
        rows = sequence(m)
        mid = hin[rows, :].astype(F32) + exchanged(0, m)
        middle[rows, :] = mid
        normal = (mid * rms_factor(mid) * gf_ref[...]).astype(BF16)
        ffn_in[rows, :] = normal
        for j in range(0, FF, 512):
            cols = slice(j, j + 512)
            gate = dot(normal, wg_ref[:, cols])
            up = dot(normal, wu_ref[:, cols])
            gates[rows, cols] = gate.astype(BF16)
            ups[rows, cols] = up.astype(BF16)
            hidden[rows, cols] = (gate * jax.nn.sigmoid(gate) * up).astype(BF16)
        snd[1, rows, :] = dot(hidden[rows, :], wd_ref[...]).astype(BF16)
        exchange(1, m).start()

    def finish(m):
        rows = sequence(m)
        act_stage[rows, :] = (middle[rows, :] + exchanged(1, m)).astype(BF16)

        @pl.when(section == 0)
        def _():
            pass_on(act_stage, hin, hin_sem, m, 0).start()

        start_emit(act_stage, act_ref, 0, m)

    def forward_tick(i, carry):
        @pl.when(i < SEQS)
        def _():
            attention(i)

        @pl.when(i >= 2)
        def _():
            finish(i - 2)

        @pl.when((i >= 1) & (i <= SEQS))
        def _():
            feed_forward(i - 1)

        return carry

    lax.fori_loop(0, SEQS + 2, forward_tick, 0)

    def feed_forward_back(m):
        rows = sequence(m)
        wait_rows(cot_ref, gin, gin_sem, m, 1)

        @pl.when(section == 0)
        def _():
            pass_on(ig_stage, gin, gin_sem, m, 1).wait_recv()

        down_in = gin[rows, :]
        total = jnp.zeros((LEN, WIDTH), F32)
        for j in range(0, FF, 512):
            cols = slice(j, j + 512)
            back = dot_nt(down_in, wd_ref[cols, :])
            gate = gates[rows, cols].astype(F32)
            up = ups[rows, cols].astype(F32)
            sig = jax.nn.sigmoid(gate)
            gate_back = (back * up * sig * (1.0 + gate * (1.0 - sig))).astype(BF16)
            up_back = (back * gate * sig).astype(BF16)
            gates[rows, cols] = gate_back
            ups[rows, cols] = up_back
            total += dot_nt(gate_back, wg_ref[:, cols]) + dot_nt(up_back, wu_ref[:, cols])
        snd[2, rows, :] = total.astype(BF16)
        exchange(2, m).start()

    def attention_back(m):
        rows = sequence(m)
        back = exchanged(2, m)
        mid = middle[rows, :]
        factor = rms_factor(mid)
        gain_acc[0:1, :] += jnp.sum(back * mid * factor, axis=0, keepdims=True)
        mid_back = gin[rows, :].astype(F32) + norm_back(mid, factor, back * gf_ref[...])
        middle[rows, :] = mid_back
        low = mid_back.astype(BF16)
        attn_in[rows, :] = low
        mixed_back = dot_nt(low, wo_ref[...]).astype(BF16)
        query, key, value = qs[rows, :], ks[rows, :], vs[rows, :]
        query_turn, key_turn = qr[rows, :], kr[rows, :]
        cosine, sine = cos_ref[:, :HEAD], sin_ref[:, :HEAD]
        query_out, key_out, value_out = [], [], []
        for g in range(GROUPS):
            cols = slice(g * HEAD, (g + 1) * HEAD)
            prob = probs[m, g]
            prob_f = prob.astype(F32)
            out_back = stacked(mixed_back, g)
            value_out.append(dot_tn(prob, out_back).astype(BF16))
            prob_back = dot_nt(out_back, value[:, cols])
            score_back = (
                prob_f * (prob_back - jnp.sum(prob_back * prob_f, axis=-1, keepdims=True))
            ).astype(BF16)
            both = jnp.concatenate([key[:, cols], key_turn[:, cols]], axis=1)
            turned = dot(score_back, both) * HEAD**-0.5
            for j in range(3):
                one = turned[j * LEN:(j + 1) * LEN]
                query_out.append((one[:, :HEAD] * cosine - one[:, HEAD:] * sine).astype(BF16))
            both = jnp.concatenate([stacked(query, g), stacked(query_turn, g)], axis=1)
            one = dot_tn(score_back, both) * HEAD**-0.5
            key_out.append((one[:, :HEAD] * cosine - one[:, HEAD:] * sine).astype(BF16))
        query_back = jnp.concatenate(query_out, axis=1)
        key_back = jnp.concatenate(key_out, axis=1)
        value_back = jnp.concatenate(value_out, axis=1)
        qkv_back[rows, :QW + 2 * KW] = jnp.concatenate([query_back, key_back, value_back], axis=1)
        snd[3, rows, :] = (
            dot_nt(query_back, wq_ref[...])
            + dot_nt(key_back, wk_ref[...])
            + dot_nt(value_back, wv_ref[...])
        ).astype(BF16)
        exchange(3, m).start()

    def finish_back(m):
        rows = sequence(m)
        back = exchanged(3, m)
        h = hin[rows, :].astype(F32)
        factor = rms_factor(h)
        gain_acc[1:2, :] += jnp.sum(back * h * factor, axis=0, keepdims=True)
        ig_stage[rows, :] = (
            middle[rows, :] + norm_back(h, factor, back * ga_ref[...])
        ).astype(BF16)

        @pl.when(section == 1)
        def _():
            pass_on(ig_stage, gin, gin_sem, m, 1).start()

        start_emit(ig_stage, ig_ref, 1, m)

    def backward_tick(i, carry):
        @pl.when(i < SEQS)
        def _():
            feed_forward_back(i)

        @pl.when(i >= 2)
        def _():
            finish_back(i - 2)

        @pl.when((i >= 1) & (i <= SEQS))
        def _():
            attention_back(i - 1)

        return carry

    lax.fori_loop(0, SEQS + 2, backward_tick, 0)

    def flush(out, slot, col):
        return pltpu.make_async_copy(
            g_stage.at[slot], out.at[:, pl.ds(col, 128)], g_sem.at[slot]
        )

    def product(left, right, right_col, out, col, count):
        def step(j, carry):
            slot = lax.rem(j, 2)

            @pl.when(j >= 2)
            def _():
                flush(out, slot, 0).wait()

            start = pl.multiple_of(j * 128, 128)
            g_stage[slot] = dot(left[...], right[:, pl.ds(right_col + start, 128)]).astype(BF16)
            flush(out, slot, pl.multiple_of(col + start, 128)).start()
            return carry

        lax.fori_loop(0, count, step, 0)
        flush(out, 0, 0).wait()
        flush(out, 1, 0).wait()

    def features(source):
        xt[...] = dot_nt(place_ref[...], source[...]).astype(BF16)

    features(gin)
    product(xt, hidden, 0, g0_ref, 0, 12)
    features(ffn_in)
    product(xt, gates, 0, g1_ref, 0, 12)
    product(xt, ups, 0, g2_ref, 0, 12)
    features(attn_in)
    product(xt, mixed, 0, g3_ref, 0, 4)
    gains = jnp.concatenate(
        [jnp.zeros((64, WIDTH), F32), gain_acc[...], jnp.zeros((56, WIDTH), F32)], axis=0
    ).astype(BF16)
    g_stage[0] = (dot(xt[...], mixed[:, 512:640]) + dot_nt(place_ref[...], gains)).astype(BF16)
    flush(g3_ref, 0, 512).start()
    flush(g3_ref, 0, 512).wait()
    features(normed)
    product(xt, qkv_back, 0, g3_ref, 640, 8)

    def drain(m, carry):
        for phase in range(4):
            exchange(phase, m).wait_send()
        for s, (source, target, sem) in enumerate(((x_ref, hin, hin_sem), (cot_ref, gin, gin_sem))):
            @pl.when((section == s) & (shard == 1))
            def _():
                fetch(source, target, sem, m)[1]().wait_send()

        @pl.when(section == 0)
        def _():
            pass_on(act_stage, hin, hin_sem, m, 0).wait_send()

        @pl.when(section == 1)
        def _():
            pass_on(ig_stage, gin, gin_sem, m, 1).wait_send()

        for which, (stage, target) in enumerate(((act_stage, act_ref), (ig_stage, ig_ref))):
            local, push = emit(stage, target, which, m)

            @pl.when(shard == 0)
            def _():
                local().wait()

            @pl.when(shard == 1)
            def _():
                push().wait()

        return carry

    lax.fori_loop(0, SEQS, drain, 0)


def reduce_kernel(g0, g1, g2, g3, o0, o1, o2, o3, *scratch):
    outs = (o0, o1, o2, o3)
    rep = lax.axis_index("replica")
    y, z, x = lax.div(rep, 2 * RING), lax.rem(lax.div(rep, RING), 2), lax.rem(rep, RING)

    def device(yy, zz, xx):
        return {"replica": (yy * 2 + zz) * RING + xx}

    def step(v, by):
        return lax.rem(v + by + RING, RING)

    near = {
        "y": (device(step(y, 1), z, x), device(step(y, -1), z, x), y),
        "x": (device(y, z, step(x, 1)), device(y, z, step(x, -1)), x),
    }
    side = device(y, 1 - z, x)

    barrier = pltpu.get_barrier_semaphore()
    for target in (near["y"][0], near["y"][1], near["x"][0], near["x"][1], side):
        pl.semaphore_signal(barrier, inc=1, device_id=target, device_id_type=MESH)
    pl.semaphore_wait(barrier, 5)

    count = len(BLOCKS)
    send, recv, here = scratch[-3:]
    buffers = [scratch[12 * b:12 * (b + 1)] for b in range(count)]
    gs = (g0, g1, g2, g3)

    def remote(b, k, source, target, to):
        return pltpu.make_async_remote_copy(
            source, target, send.at[b, k], recv.at[b, k], device_id=to, device_id_type=MESH
        )

    def make(b):
        part, col, wide, cut = BLOCKS[b]
        axis = PARTS[part][1]
        other = "x" if axis == "y" else "y"
        right, left, me = near[axis]
        right2, left2, me2 = near[other]
        r1a, r1b, r2l, r2r, c1, c2, h, s1a, s1b, t2l, t2r, zz = buffers[b]
        zs, zr = zz.at[0:PIECE], zz.at[PIECE:PIECE + 48]
        fa, fb = pl.ds(0, cut), pl.ds(cut, wide - cut)
        ga, gb, gw = pl.ds(col, cut), pl.ds(col + cut, wide - cut), pl.ds(col, wide)
        g = gs[part]

        def chunk(by, cols):
            t = step(me, by)
            return g.at[t, :, :, cols] if axis == "y" else g.at[:, t, :, cols]

        plus2, minus2 = step(me2, 1), step(me2, -1)
        far2 = step(me2, 2)
        first = [
            remote(b, 0, chunk(2, ga), r1a, right),
            remote(b, 1, chunk(2, gb), r1b, left),
            remote(b, 2, chunk(1, gb), r2l.at[:, :, fb], right),
            remote(b, 3, chunk(-1, ga), r2r.at[:, :, fa], left),
        ]
        locals_ = [
            pltpu.make_async_copy(chunk(1, ga), c1, here.at[b, 0]),
            pltpu.make_async_copy(chunk(-1, gb), c2, here.at[b, 1]),
            pltpu.make_async_copy(chunk(0, gw), h, here.at[b, 2]),
        ]
        second = [
            remote(b, 4, c1, r2l.at[:, :, fa], right),
            remote(b, 5, c2, r2r.at[:, :, fb], left),
        ]
        third = [
            remote(b, 6, h.at[far2, :, fa], s1a, right2),
            remote(b, 7, h.at[far2, :, fb], s1b, left2),
            remote(b, 8, h.at[plus2, :, fb], t2l.at[:, fb], right2),
            remote(b, 9, h.at[minus2, :, fa], t2r.at[:, fa], left2),
        ]
        fourth = [
            remote(b, 10, h.at[plus2, :, fa], t2l.at[:, fa], right2),
            remote(b, 11, h.at[minus2, :, fb], t2r.at[:, fb], left2),
        ]
        fifth = [
            remote(b, 12, zz.at[pl.ds(pl.multiple_of(32 * (1 - z), 16), 48)], zr, side),
        ]

        def run_a():
            for copy in first + locals_:
                copy.start()

        def run_b():
            first[0].wait_recv()
            locals_[0].wait()
            c1[...] = (c1[...].astype(F32) + r1a[...].astype(F32)).astype(BF16)
            second[0].start()
            first[1].wait_recv()
            locals_[1].wait()
            c2[...] = (c2[...].astype(F32) + r1b[...].astype(F32)).astype(BF16)
            second[1].start()

        def run_c():
            for copy in first[2:] + second:
                copy.wait_recv()
            locals_[2].wait()
            h[...] = (
                h[...].astype(F32) + r2l[...].astype(F32) + r2r[...].astype(F32)
            ).astype(BF16)
            for copy in third:
                copy.start()

        def run_d():
            third[0].wait_recv()
            h[plus2, :, 0:cut] = (
                h[plus2, :, 0:cut].astype(F32) + s1a[...].astype(F32)
            ).astype(BF16)
            fourth[0].start()
            third[1].wait_recv()
            h[minus2, :, cut:wide] = (
                h[minus2, :, cut:wide].astype(F32) + s1b[...].astype(F32)
            ).astype(BF16)
            fourth[1].start()

        def run_e():
            for copy in third[2:] + fourth:
                copy.wait_recv()
            zz[0:PIECE] = (
                h[me2].astype(F32) + t2l[...].astype(F32) + t2r[...].astype(F32)
            ).astype(BF16)
            fifth[0].start()

        def run_f():
            fifth[0].wait_recv()
            mine = zz[0:PIECE].astype(F32)
            theirs = zz[PIECE:PIECE + 48].astype(F32)
            low = z == 0
            outs[part][:, col:col + wide] = jnp.where(
                low, mine[0:40] + theirs[0:40], mine[40:80] + theirs[8:48]
            )

        def finish():
            for copy in first + second + third + fourth + fifth:
                copy.wait_send()

        return (run_a, run_f, run_e, run_d, run_c, run_b, finish)

    made = [make(b) for b in range(count)]
    for t in range(count + 5):
        for which, late in ((0, 0), (1, 5), (2, 4), (3, 3), (4, 2), (5, 1)):
            if 0 <= t - late < count:
                made[t - late][which]()
    for b in range(count):
        made[b][6]()


def on_device(x, cot, ga, wq, wk, wv, wo, gf, wg, wu, wd):
    cosine, sine = rope_tables()
    vmem = pl.BlockSpec(memory_space=pltpu.VMEM)
    any_ = pl.BlockSpec(memory_space=pl.ANY)
    sds = jax.ShapeDtypeStruct
    rows = (TOKENS, WIDTH)
    dma = pltpu.SemaphoreType.DMA
    outs = pl.pallas_call(
        compute_kernel,
        out_shape=[sds(x.shape, BF16)] * 2 + [sds((ROWS, part[0]), BF16) for part in PARTS],
        in_specs=[any_] * 2 + [vmem] * 13,
        out_specs=[any_] * 6,
        scratch_shapes=[
            pltpu.VMEM((WIDTH, QW), BF16),
            pltpu.VMEM((WIDTH, KW), BF16),
            pltpu.VMEM(rows, BF16),
            pltpu.VMEM(rows, BF16),
            pltpu.VMEM(rows, BF16),
            pltpu.VMEM((TOKENS, QW), BF16),
            pltpu.VMEM((TOKENS, QW), BF16),
            pltpu.VMEM((TOKENS, KW), BF16),
            pltpu.VMEM((TOKENS, KW), BF16),
            pltpu.VMEM((TOKENS, KW), BF16),
            pltpu.VMEM((SEQS, GROUPS, 3 * LEN, LEN), BF16),
            pltpu.VMEM((TOKENS, 640), BF16),
            pltpu.VMEM(rows, F32),
            pltpu.VMEM(rows, BF16),
            pltpu.VMEM((TOKENS, FF), BF16),
            pltpu.VMEM((TOKENS, FF), BF16),
            pltpu.VMEM((TOKENS, FF), BF16),
            pltpu.VMEM(rows, BF16),
            pltpu.VMEM((TOKENS, 1024), BF16),
            pltpu.VMEM((8, WIDTH), F32),
            pltpu.VMEM((ROWS, TOKENS), BF16),
            pltpu.VMEM((4,) + rows, BF16),
            pltpu.VMEM((4,) + rows, BF16),
            pltpu.VMEM(rows, BF16),
            pltpu.VMEM(rows, BF16),
            pltpu.VMEM((2, ROWS, 128), BF16),
            dma((SEQS,)),
            dma((SEQS,)),
            dma((SEQS,)),
            dma((SEQS,)),
            dma((4, SEQS)),
            dma((4, SEQS)),
            dma((2, SEQS)),
            dma((2, SEQS)),
            dma((2, SEQS)),
            dma((2,)),
        ],
        compiler_params=pltpu.CompilerParams(
            collective_id=0, has_side_effects=True, vmem_limit_bytes=63 * 2**20
        ),
        cost_estimate=pl.CostEstimate(
            flops=26 * 10**9, bytes_accessed=36 * 10**6, transcendentals=10**7
        ),
        name="layer",
    )(
        x, cot, ga, wq[0], wk[0], wv[0], wo[0], gf, wg[0], wu[0], wd[0],
        jnp.asarray(cosine), jnp.asarray(sine),
        jnp.asarray(turn_matrix(), BF16), jnp.asarray(place_matrix(), BF16),
    )
    acts, grads, *gs = outs
    buffers = []
    for part, col, wide, cut in BLOCKS:
        rest = wide - cut
        buffers += [
            pltpu.VMEM((RING, PIECE, cut), BF16),
            pltpu.VMEM((RING, PIECE, rest), BF16),
            pltpu.VMEM((RING, PIECE, wide), BF16),
            pltpu.VMEM((RING, PIECE, wide), BF16),
            pltpu.VMEM((RING, PIECE, cut), BF16),
            pltpu.VMEM((RING, PIECE, rest), BF16),
            pltpu.VMEM((RING, PIECE, wide), BF16),
            pltpu.VMEM((PIECE, cut), BF16),
            pltpu.VMEM((PIECE, rest), BF16),
            pltpu.VMEM((PIECE, wide), BF16),
            pltpu.VMEM((PIECE, wide), BF16),
            pltpu.VMEM((PIECE + 48, wide), BF16),
        ]
    n = len(BLOCKS)
    down, gate, up, mix = pl.pallas_call(
        reduce_kernel,
        out_shape=[sds((40, part[0]), F32) for part in PARTS],
        in_specs=[any_] * 4,
        out_specs=[vmem] * 4,
        scratch_shapes=buffers + [dma((n, 13)), dma((n, 13)), dma((n, 3))],
        compiler_params=pltpu.CompilerParams(
            collective_id=1, has_side_effects=True, vmem_limit_bytes=60 * 2**20
        ),
        name="reduce",
    )(*[g.reshape(RING, RING, PIECE, part[0]) for g, part in zip(gs, PARTS)])
    mix = mix[:OWN]
    return (
        acts[None],
        grads[None],
        mix[:, QW + 1][None],
        mix[:, 640:640 + QW][None],
        mix[:, 640 + QW:640 + QW + KW][None],
        mix[:, 640 + QW + KW:640 + QW + 2 * KW][None],
        mix[:, :QW].T[None],
        mix[:, QW][None],
        gate[:OWN][None],
        up[:OWN][None],
        down[:OWN].T[None],
    )


def solution(mesh):
    in_specs = (
        P("replica", None, None),
        P("replica", None, None),
        P("section", None),
        P("section", None, "shard"),
        P("section", None, "shard"),
        P("section", None, "shard"),
        P("section", "shard", None),
        P("section", None),
        P("section", None, "shard"),
        P("section", None, "shard"),
        P("section", "shard", None),
    )
    out_specs = (
        P("section", "replica", None, None),
        P("section", "replica", None, None),
        P("section", "replica"),
        P("section", "replica", "shard"),
        P("section", "replica", "shard"),
        P("section", "replica", "shard"),
        P("section", "shard", "replica"),
        P("section", "replica"),
        P("section", "replica", "shard"),
        P("section", "replica", "shard"),
        P("section", "shard", "replica"),
    )
    return jax.shard_map(
        on_device, mesh=mesh, in_specs=in_specs, out_specs=out_specs, check_vma=False
    )
```

time: 1420 us -> 321 us (0.23); the launches traced: 1400 us -> 320 us
  waiting for transfers between devices: 524 us -> 0 us
  Pallas kernels: 0 us -> 301 us
  blocking collectives: 295 us -> 0 us
  matrix products: 270 us -> 0 us
  other arithmetic: 144 us -> 0 us
  local copies, waits for them, and re-layouts: 102 us -> 18 us
  starting transfers between devices: 49.9 us -> 0 us
  between operations: 18.9 us -> 0.71 us
    psum x19 -> x0, waiting for transfers between devices: 425 us -> none  [the longest x5 144 us: forward_layer(): attended = lax.psum(dense(mixed_heads, weight_o, 'lq,qd->ld'), 'shard')]
    pallas_call x0 -> x2, Pallas kernels: none -> 301 us  [the longest x1 205 us: on_device(): pl.pallas_call(compute_kernel, out_shape=[sds(x.shape, BF16)] * 2 + [sds(...]
    unnamed x2 -> x0, blocking collectives: 295 us -> none
    dot_general x140 -> x0, matrix products: 270 us -> none  [dense(): return jnp.einsum(form, left, right, preferred_element_type=jnp.float32)]
    unnamed x29 -> x0, waiting for transfers between devices: 97.9 us -> none
    unnamed x423 -> x22, local copies, waits for them, and re-layouts: 58.4 us -> 13.4 us
    unnamed x26 -> x0, other arithmetic: 42.5 us -> none
    convert_element_type x5 -> x0, local copies, waits for them, and re-layouts: 37.5 us -> none  [the longest x1 16.5 us: on_device(): ffn_sums[3][None].astype(jnp.bfloat16)]
  transfers between devices with their start and end apart: 36 -> 0, of which waited for: 20 -> 0; matrix products, arithmetic and copies ran while one was open for 31% -> 0% of each run, Pallas kernels for 0% -> 0%
where the time goes in v1:
time: 321 us; the launch traced here: 320 us
  Pallas kernels  301 us (94%)
  local copies, waits for them, and re-layouts  18 us (6%)
    pallas_call x1, Pallas kernels, on_device(): pl.pallas_call(compute_kernel, out_shape=[sds(x.shape, BF16)] * 2 + [sds(...  205 us
    pallas_call x1, Pallas kernels, on_device(): pl.pallas_call(reduce_kernel, out_shape=[sds((40, part[0]), F32) for part...  96.1 us
    unnamed x22, local copies, waits for them, and re-layouts  13.4 us

profile of v1, /device:TPU:0, one launch (start us, length us, event | category | flops | bytes accessed | tf_op | source)
XLA Modules:
  0.0 320.0 jit_solution(13037444552527794798)
XLA Ops:
  0.6 0.0 copy-start
  0.7 2.2 copy.37
  2.8 2.1 copy.38
  4.9 0.0 copy-done
  4.9 1.6 copy.36
  6.5 205.2 %layer.1 = (bf16[4,128,1152]{2,1,0:T(8,128)(2,1)}, bf16[4,128,1152]{2,1,0:T(8,128)(2,1)}, bf16[1280,1536]{1,0:T(8,128)(2,1)}, bf16[1280,1536]{1,0:T(8,128)(2,1)}...) custom-call(bf16[4,128,1152]{2,1,0:T(8,128)(2,1)} %x_ref.1, bf16[4,128,1152]{2,1,0:T(8,128)(2,1)} %cot_ref.1, ...), custom_call_target="tpu_custom_call" | custom-call | flops 25999998976 | bytes 36000000 | tf_op jit(solution)/shard_map/layer/pallas_call | solution.py:628
  211.7 96.1 %reduce.5 = (f32[40,1536]{1,0:T(8,128)}, f32[40,1536]{1,0:T(8,128)}, f32[40,1536]{1,0:T(8,128)}, f32[40,1664]{1,0:T(8,128)}) custom-call(bf16[4,4,80,1536]{3,2,1,0:T(8,128)(2,1)} %bitcast.34, bf16[4,4,80,1536]{3,2,1,0:T(8,128)(2,1)} %bitcast.35, bf16[4,4,80,1536]{3,2,1,0:T(8,128)(2,1)} %bitcast.36, bf16[4,4,80,1664]{3,2,1,0:T(8,128)(2,1)} %bitcast.33), custom_call_target="tpu_custom_call" | custom-call | tf_op jit(solution)/shard_map/reduce/pallas_call | solution.py:702
  307.8 0.0 copy-start.3
  307.8 0.0 copy-start.4
  307.8 1.0 slice_bitcast_fusion.2
  308.8 0.9 copy.43
  309.7 1.5 slice_reduce_fusion
  311.3 1.0 slice_bitcast_fusion.5
  312.2 0.0 copy-start.2
  312.2 1.1 slice_bitcast_fusion.3
  313.3 0.7 copy.42
  314.0 0.7 copy.41
  314.7 0.7 copy.40
  315.3 0.7 copy.39
  316.1 0.0 copy-done.3
  316.1 0.0 copy-done.4
  316.1 0.9 copy.45
  317.0 0.0 copy-start.1
  317.0 0.9 copy.44
  318.0 0.0 copy-done.2
  318.0 1.0 copy.48
  319.0 0.0 copy-done.1
  319.0 1.0 copy.49
  (1 shorter events, 0.0 us)
Async XLA Ops:
  0.6 4.3 %copy-start = (bf16[1,1152,576]{1,2,0:T(8,128)(2,1)S(1)}, bf16[1,1152,576]{1,2,0:T(8,128)(2,1)}, u32[]{:S(2)}) copy-start(bf16[1,1152,576]{1,2,0:T(8,128)(2,1)} %param.18) | copy-start | bytes 3981316
  307.8 8.3 %copy-start.3 = (f32[40,1536]{1,0:T(8,128)S(1)}, f32[40,1536]{1,0:T(8,128)}, u32[]{:S(2)}) copy-start(f32[40,1536]{1,0:T(8,128)} %get-tuple-element.30) | copy-start | bytes 737284
  307.8 8.3 %copy-start.4 = (f32[40,1536]{1,0:T(8,128)S(1)}, f32[40,1536]{1,0:T(8,128)}, u32[]{:S(2)}) copy-start(f32[40,1536]{1,0:T(8,128)} %get-tuple-element.29) | copy-start | bytes 737284
  312.2 5.7 %copy-start.2 = (bf16[4,128,1152]{2,1,0:T(8,128)(2,1)S(1)}, bf16[4,128,1152]{2,1,0:T(8,128)(2,1)}, u32[]{:S(2)}) copy-start(bf16[4,128,1152]{2,1,0:T(8,128)(2,1)} %get-tuple-element.21) | copy-start | bytes 3538948
  317.0 1.9 copy-start.1

commit v2 on v1

v2 whole, which is shorter than its diff:
```python
import jax
import jax.numpy as jnp
import numpy as np
from jax import lax
from jax.experimental import pallas as pl
from jax.experimental.pallas import tpu as pltpu
from jax.sharding import PartitionSpec as P

HEAD = 64
HEADS = 9
GROUPS = 3
WIDTH = 1152
FF = 1536
LEN = 128
SEQS = 4
TOKENS = LEN * SEQS
QW = HEADS * HEAD
KW = GROUPS * HEAD
RING = 4
PIECE = 80
ROWS = RING * RING * PIECE
OWN = WIDTH // 32
EPSILON = 1e-05
ROPE_BASE = 10000.0
F32 = jnp.float32
BF16 = jnp.bfloat16
MESH = pl.DeviceIdType.MESH
PARTS = (1536, 1536, 1536, 1664)
BLOCKS = (
    (0, 0, 768, 384, "x"),
    (0, 768, 768, 384, "y"),
    (1, 0, 768, 384, "x"),
    (1, 768, 768, 384, "y"),
    (2, 0, 768, 384, "x"),
    (2, 768, 768, 384, "y"),
    (3, 0, 640, 384, "y"),
    (3, 640, 512, 256, "x"),
    (3, 1152, 256, 128, "x"),
    (3, 1408, 256, 128, "y"),
)
COUNT = len(BLOCKS)
COLUMNS = sum(PARTS)
WIDE = max(block[2] for block in BLOCKS)
C_SLOTS, L_SLOTS, H_SLOTS, G_SLOTS = 7, 4, 5, 4


def dot(left, right):
    return lax.dot_general(left, right, (((1,), (0,)), ((), ())), preferred_element_type=F32)


def dot_nt(left, right):
    return lax.dot_general(left, right, (((1,), (1,)), ((), ())), preferred_element_type=F32)


def dot_tn(left, right):
    return lax.dot_general(left, right, (((0,), (0,)), ((), ())), preferred_element_type=F32)


def rope_tables():
    half = HEAD // 2
    position = np.arange(LEN, dtype=np.float32)
    frequency = (ROPE_BASE ** (-np.arange(half, dtype=np.float32) * 2.0 / HEAD)).astype(np.float32)
    angles = position[:, None] * frequency[None, :]
    cosine = np.cos(angles).astype(np.float32)
    sine = np.sin(angles).astype(np.float32)
    return (
        np.tile(np.concatenate([cosine, cosine], 1), (1, 2)),
        np.tile(np.concatenate([sine, sine], 1), (1, 2)),
    )


def turn_matrix():
    turn = np.zeros((128, 128), np.float32)
    for head in range(2):
        for j in range(HEAD // 2):
            first, second = head * HEAD + j, head * HEAD + HEAD // 2 + j
            turn[second, first] = -1.0
            turn[first, second] = 1.0
    return turn


def place_matrix():
    place = np.zeros((RING, RING, PIECE, WIDTH), np.float32)
    for y in range(RING):
        for x in range(RING):
            for z in range(2):
                owner = (y * 2 + z) * RING + x
                for i in range(OWN):
                    place[y, x, z * 40 + i, owner * OWN + i] = 1.0
    return place.reshape(ROWS, WIDTH)


def rms_factor(rows):
    return lax.rsqrt(jnp.mean(rows * rows, axis=-1, keepdims=True) + EPSILON)


def norm_back(rows, factor, grad):
    return factor * grad - rows * factor**3 * jnp.mean(grad * rows, axis=-1, keepdims=True)


def rows_of(first, count):
    return pl.ds(pl.multiple_of(first * LEN, LEN), count * LEN)


class Ring:
    def __init__(self, gs, outs, r2l, r2r, r1, cs, hs, ls, rs, second, send, recv, here):
        self.gs, self.outs, self.r2l, self.r2r = gs, outs, r2l, r2r
        self.r1, self.cs, self.hs, self.ls, self.rs = r1, cs, hs, ls, rs
        self.second, self.send, self.recv, self.here = second, send, recv, here
        rep = lax.axis_index("replica")
        y, z, x = lax.div(rep, 2 * RING), lax.rem(lax.div(rep, RING), 2), lax.rem(rep, RING)
        self.z = z

        def device(yy, zz, xx):
            return {"replica": (yy * 2 + zz) * RING + xx}

        self.near = {
            "y": (device(self.turn(y, 1), z, x), device(self.turn(y, -1), z, x), y),
            "x": (device(y, z, self.turn(x, 1)), device(y, z, self.turn(x, -1)), x),
        }
        self.side = device(y, 1 - z, x)
        self.made = [self.make(b) for b in range(COUNT)]
        self.sent = set()
        self.steps = dict(
            a=self.a, b0=self.b0, b=self.b, c0=self.c0, c=self.c, d=self.d, e=self.e, f=self.f
        )

    @staticmethod
    def turn(v, by):
        return lax.rem(v + by + RING, RING)

    def neighbours(self):
        return self.near["y"][:2] + self.near["x"][:2]

    def make(self, b):
        part, col, wide, cut, axis = BLOCKS[b]
        base = sum(block[2] for block in BLOCKS[:b])
        right, left, me = self.near[axis]
        right2, left2, me2 = self.near["x" if axis == "y" else "y"]
        r1a, r1b = self.r1[2 * b:2 * b + 2]
        s1a, s1b, t2l, t2r, zz = self.second[5 * b:5 * b + 5]
        cs, ls, rs, hs = b % C_SLOTS, b % L_SLOTS, b % L_SLOTS, b % H_SLOTS
        c = self.cs.at[cs]
        r2l, r2r = self.r2l, self.r2r
        rest = wide - cut
        g = self.gs[part]

        def remote(k, source, target, to):
            return pltpu.make_async_remote_copy(
                source, target, self.send.at[b, k], self.recv.at[b, k],
                device_id=to, device_id_type=MESH,
            )

        def load(k, source, target):
            return pltpu.make_async_copy(source, target, self.here.at[b, k])

        def chunk(by, first, count):
            t = self.turn(me, by)
            cols = pl.ds(col + first, count)
            return g.at[t, :, :, cols] if axis == "y" else g.at[:, t, :, cols]

        def lanes(ref, first, count):
            return ref.at[:, :, pl.ds(first, count)]

        plus2, minus2, far2 = self.turn(me2, 1), self.turn(me2, -1), self.turn(me2, 2)
        fa, fb = pl.ds(0, cut), pl.ds(cut, rest)
        early = dict(
            first=[
                remote(0, chunk(2, 0, cut), r1a, right),
                remote(1, chunk(2, cut, rest), r1b, left),
                remote(2, chunk(1, cut, rest), lanes(r2l, base + cut, rest), right),
                remote(3, chunk(-1, 0, cut), lanes(r2r, base, cut), left),
            ],
            near=[
                load(0, chunk(1, 0, cut), lanes(c, 0, cut)),
                load(1, chunk(-1, cut, rest), lanes(c, cut, rest)),
            ],
        )
        if self.hs is None:
            return early
        l, r, h = self.ls.at[ls], self.rs.at[rs], self.hs.at[hs]
        return dict(
            early,
            second=[
                remote(4, lanes(c, 0, cut), lanes(r2l, base, cut), right),
                remote(5, lanes(c, cut, rest), lanes(r2r, base + cut, rest), left),
            ],
            back=[
                load(2, chunk(0, 0, wide), lanes(h, 0, wide)),
                load(3, lanes(r2l, base, wide), lanes(l, 0, wide)),
                load(4, lanes(r2r, base, wide), lanes(r, 0, wide)),
            ],
            third=[
                remote(6, h.at[far2, :, fa], s1a, right2),
                remote(7, h.at[far2, :, fb], s1b, left2),
                remote(8, h.at[plus2, :, fb], t2l.at[:, fb], right2),
                remote(9, h.at[minus2, :, fa], t2r.at[:, fa], left2),
            ],
            fourth=[
                remote(10, h.at[plus2, :, fa], t2l.at[:, fa], right2),
                remote(11, h.at[minus2, :, fb], t2r.at[:, fb], left2),
            ],
            fifth=[
                remote(
                    12,
                    zz.at[pl.ds(pl.multiple_of(32 * (1 - self.z), 16), 48)],
                    zz.at[pl.ds(PIECE, 48)],
                    self.side,
                ),
            ],
        )

    def settle(self, b, *names):
        for name in names:
            if (b, name) not in self.sent:
                self.sent.add((b, name))
                for copy in self.made[b][name]:
                    copy.wait_send()

    def a(self, b):
        for copy in self.made[b]["first"]:
            copy.start()

    def b0(self, b):
        if b >= C_SLOTS:
            self.settle(b - C_SLOTS, "second")
        for copy in self.made[b]["near"]:
            copy.start()

    def b(self, b):
        _, _, wide, cut, _ = BLOCKS[b]
        m = self.made[b]
        slot = b % C_SLOTS
        for k, (first, last) in enumerate(((0, cut), (cut, wide))):
            m["first"][k].wait_recv()
            m["near"][k].wait()
            self.cs[slot, :, :, first:last] = (
                self.cs[slot, :, :, first:last] + self.r1[2 * b + k][...]
            )
            m["second"][k].start()

    def c0(self, b):
        if b >= H_SLOTS:
            self.settle(b - H_SLOTS, "third", "fourth")
        m = self.made[b]
        for copy in m["first"][2:] + m["second"]:
            copy.wait_recv()
        for copy in m["back"]:
            copy.start()

    def c(self, b):
        wide = BLOCKS[b][2]
        m = self.made[b]
        for copy in m["back"]:
            copy.wait()
        slot, side = b % H_SLOTS, b % L_SLOTS
        total = self.hs[slot, :, :, 0:wide] + (
            self.ls[side, :, :, 0:wide] + self.rs[side, :, :, 0:wide]
        )
        self.hs[slot, :, :, 0:wide] = total
        for copy in m["third"]:
            copy.start()

    def d(self, b):
        _, _, wide, cut, axis = BLOCKS[b]
        m = self.made[b]
        me2 = self.near["x" if axis == "y" else "y"][2]
        slot = b % H_SLOTS
        for k, (by, first, last) in enumerate(((1, 0, cut), (-1, cut, wide))):
            t = self.turn(me2, by)
            m["third"][k].wait_recv()
            self.hs[slot, t, :, first:last] = (
                self.hs[slot, t, :, first:last] + self.second[5 * b + k][...]
            )
            m["fourth"][k].start()

    def e(self, b):
        _, _, wide, _, axis = BLOCKS[b]
        m = self.made[b]
        me2 = self.near["x" if axis == "y" else "y"][2]
        t2l, t2r, zz = self.second[5 * b + 2:5 * b + 5]
        for copy in m["third"][2:] + m["fourth"]:
            copy.wait_recv()
        total = self.hs[b % H_SLOTS, me2, :, 0:wide] + (t2l[...] + t2r[...])
        zz[0:PIECE] = total
        m["fifth"][0].start()

    def f(self, b):
        part, col, wide, _, _ = BLOCKS[b]
        self.made[b]["fifth"][0].wait_recv()
        zz = self.second[5 * b + 4]
        mine = zz[0:PIECE].astype(F32)
        theirs = zz[PIECE:PIECE + 48].astype(F32)
        self.outs[part][:, col:col + wide] = jnp.where(
            self.z == 0, mine[0:40] + theirs[0:40], mine[40:80] + theirs[8:48]
        )

    def finish(self):
        for b in range(COUNT):
            self.settle(b, "first", "second", "third", "fourth", "fifth")

    def run(self, *words):
        for word in words:
            self.steps[word[:-1]](int(word[-1]))


def layer_kernel(
    x_ref, cot_ref, ga_ref, gf_ref,
    wq_in, wk_in, wv_in, wo_in, cos_in, sin_in, turn_in, wg_in, wu_in, wd_in, place_in,
    act_ref, ig_ref, g0, g1, g2, g3, r2l, r2r, o0, o1, o2, o3,
    *scratch,
):
    (
        wq_ref, wk_ref, wv_ref, wo_ref, cos_ref, sin_ref, turn_ref, wd_ref, place_ref,
        hin, gin, normed, qs, ks, vs, probs, mixed, middle, ffn_in, gates, ups, hidden,
        qkv_back, gain_acc, xt, middle_back, snd_a, rcv_a, snd_b, rcv_b, g_stage, cs,
    ) = scratch[:32]
    r1 = scratch[32:32 + 2 * COUNT]
    stage2 = scratch[32 + 2 * COUNT:32 + 7 * COUNT]
    (
        load_sem, in_sem, in_send, ar_send, ar_recv, step_send, step_recv, out_sem, out_send, g_sem,
        ring_send, ring_recv, ring_here,
    ) = scratch[32 + 7 * COUNT:]
    section = lax.axis_index("section")
    shard = lax.axis_index("shard")
    rep = lax.axis_index("replica")
    zlo = lax.rem(lax.div(rep, RING), 2)
    side = rep + RING - 2 * RING * zlo
    core = {"section": 1 - section}
    twin = {"shard": 1 - shard, "replica": side}
    swap = {"replica": side}

    def make_ring(hs, ls, rs):
        return Ring(
            (g0, g1, g2, g3), (o0, o1, o2, o3), r2l, r2r, r1, cs, hs, ls, rs, stage2,
            ring_send, ring_recv, ring_here,
        )

    ring = make_ring(None, None, None)
    wide_weights = []

    loads = [
        pltpu.make_async_copy(source, target, load_sem.at[k])
        for k, (source, target) in enumerate(
            (
                (wq_in, wq_ref), (wk_in, wk_ref), (wv_in, wv_ref), (cos_in, cos_ref),
                (sin_in, sin_ref), (turn_in, turn_ref), (wo_in, wo_ref), (wd_in, wd_ref),
                (place_in, place_ref),
            )
        )
    ]
    for copy in loads[:7]:
        copy.start()

    barrier = pltpu.get_barrier_semaphore()
    near = (core, twin, swap) + ring.neighbours()
    for target in near:
        pl.semaphore_signal(barrier, inc=1, device_id=target, device_id_type=MESH)
    pl.semaphore_wait(barrier, len(near))

    inputs = ((x_ref, hin), (cot_ref, gin))

    def fetch(s, m):
        source, target = inputs[s]
        rows = rows_of(m, 1)

        def local():
            return pltpu.make_async_copy(source.at[m], target.at[rows], in_sem.at[s, m])

        def push():
            return pltpu.make_async_remote_copy(
                source.at[m], target.at[rows], in_send.at[s, m], in_sem.at[s, m],
                device_id=swap, device_id_type=MESH,
            )

        return local, push

    for m in range(SEQS):
        for s in range(2):
            local, push = fetch(s, m)

            @pl.when((section == s) & (shard == 0))
            def _():
                local().start()

            @pl.when((section == s) & (shard == 1))
            def _():
                push().start()

    for copy in loads[7:]:
        copy.start()

    def wait_input(s, m):
        local, push = fetch(s, m)

        @pl.when(shard == 0)
        def _():
            local().wait()

        @pl.when(shard == 1)
        def _():
            push().wait_recv()

    def pass_on(which, first, count, k):
        source, target = ((snd_b, hin), (snd_a, gin))[which]
        rows = rows_of(first, count)
        return pltpu.make_async_remote_copy(
            source.at[rows], target.at[rows], step_send.at[which, k], step_recv.at[which, k],
            device_id=core, device_id_type=MESH,
        )

    halves = ((snd_a, rcv_a), (snd_b, rcv_b), (snd_b, rcv_b), (snd_a, rcv_a))

    def exchange(phase, first, count, k):
        snd, rcv = halves[phase]
        rows = rows_of(first, count)
        return pltpu.make_async_remote_copy(
            snd.at[rows], rcv.at[rows], ar_send.at[phase, k], ar_recv.at[phase, k],
            device_id=twin, device_id_type=MESH,
        )

    def offer(phase, first, count, k, value):
        halves[phase][0][rows_of(first, count), :] = value.astype(BF16)
        exchange(phase, first, count, k).start()

    def exchanged(phase, first, count, k):
        exchange(phase, first, count, k).wait()
        snd, rcv = halves[phase]
        rows = rows_of(first, count)
        return snd[rows, :].astype(F32) + rcv[rows, :].astype(F32)

    def emit(which, m):
        source, target = ((snd_b, act_ref), (snd_a, ig_ref))[which]
        rows = rows_of(m, 1)

        def local():
            return pltpu.make_async_copy(source.at[rows], target.at[m], out_sem.at[which, m])

        def push():
            return pltpu.make_async_remote_copy(
                source.at[rows], target.at[m], out_send.at[which, m], out_sem.at[which, m],
                device_id=swap, device_id_type=MESH,
            )

        return local, push

    def start_emit(which, m):
        local, push = emit(which, m)

        @pl.when(shard == 0)
        def _():
            local().start()

        @pl.when(shard == 1)
        def _():
            push().start()

    def settle_emit(which, m):
        local, push = emit(which, m)

        @pl.when(shard == 0)
        def _():
            local().wait()

        @pl.when(shard == 1)
        def _():
            push().wait_send()

    gain_acc[...] = jnp.zeros_like(gain_acc)
    mixed[:, QW:] = jnp.zeros((TOKENS, 64), BF16)
    qkv_back[:, QW + 2 * KW:] = jnp.zeros((TOKENS, 64), BF16)

    def stacked(value, g):
        return jnp.concatenate(
            [value[:, (3 * g + j) * HEAD:(3 * g + j + 1) * HEAD] for j in range(3)], axis=0
        )

    def turned(value):
        wide = value.shape[1]
        return jnp.concatenate(
            [
                dot(value[:, c:min(c + 128, wide)], turn_ref[:min(128, wide - c), :min(128, wide - c)])
                for c in range(0, wide, 128)
            ],
            axis=1,
        )

    def spread(table, wide):
        return jnp.concatenate(
            [table[:, :min(128, wide - c)] for c in range(0, wide, 128)], axis=1
        )

    def rope(value):
        high = value.astype(BF16)
        low = (value - high.astype(F32)).astype(BF16)
        wide = value.shape[1]
        cosine, sine = spread(cos_ref[...], wide), spread(sin_ref[...], wide)
        return (value * cosine + (turned(high) + turned(low)) * sine).astype(BF16)

    def attention(m):
        rows = rows_of(m, 1)

        @pl.when(section == 0)
        def _():
            wait_input(0, m)

        @pl.when(section == 1)
        def _():
            pass_on(0, m, 1, m).wait_recv()

        h = hin[rows, :].astype(F32)
        normal = (h * rms_factor(h) * ga_ref[...]).astype(BF16)
        normed[rows, :] = normal
        query = rope(dot_nt(normal, wq_ref[...]))
        key = rope(dot_nt(normal, wk_ref[...]))
        value = dot_nt(normal, wv_ref[...]).astype(BF16)
        qs[rows, :] = query
        ks[rows, :] = key
        vs[rows, :] = value
        at = lax.rem(lax.broadcasted_iota(jnp.int32, (3 * LEN, LEN), 0), LEN)
        causal = at >= lax.broadcasted_iota(jnp.int32, (3 * LEN, LEN), 1)
        heads = []
        for g in range(GROUPS):
            cols = slice(g * HEAD, (g + 1) * HEAD)
            scores = dot_nt(stacked(query, g), key[:, cols]) * HEAD**-0.5
            scores = jnp.where(causal, scores, -1e30)
            top = jnp.max(scores, axis=-1, keepdims=True)
            weight = jnp.exp(scores - top)
            prob = (weight / jnp.sum(weight, axis=-1, keepdims=True)).astype(BF16)
            probs[m, g] = prob
            out = dot(prob, value[:, cols]).astype(BF16)
            heads += [out[j * LEN:(j + 1) * LEN] for j in range(3)]
        mix = jnp.concatenate(heads, axis=1)
        mixed[rows, :QW] = mix
        offer(0, m, 1, m, dot(mix, wo_ref[...]))

    def feed_forward(m):
        rows = rows_of(m, 1)
        mid = hin[rows, :].astype(F32) + exchanged(0, m, 1, m)
        middle[rows, :] = mid
        normal = (mid * rms_factor(mid) * gf_ref[...]).astype(BF16)
        ffn_in[rows, :] = normal
        for j in range(0, FF, 512):
            cols = slice(j, j + 512)
            gate = dot(normal, wide_weights[0][:, cols])
            up = dot(normal, wide_weights[1][:, cols])
            gates[rows, cols] = gate.astype(BF16)
            ups[rows, cols] = up.astype(BF16)
            hidden[rows, cols] = (gate * jax.nn.sigmoid(gate) * up).astype(BF16)

        @pl.when(section == 0)
        def _():
            offer(1, m, 1, m, dot(hidden[rows, :], wd_ref[...]))

    def finish(first, count, k):
        value = exchanged(1, first, count, k)
        rows = rows_of(first, count)
        snd_b[rows, :] = (middle[rows, :] + value).astype(BF16)

    def feed_forward_back(j):
        rows = rows_of(2 * j, 2)

        @pl.when(section == 1)
        def _():
            wait_input(1, 2 * j)
            wait_input(1, 2 * j + 1)

        @pl.when(section == 0)
        def _():
            for m in (2 * j, 2 * j + 1):
                pass_on(1, m, 1, m).wait_recv()

        down_in = gin[rows, :]
        total = jnp.zeros((2 * LEN, WIDTH), F32)
        for c in range(0, FF, 512):
            cols = slice(c, c + 512)
            back = dot_nt(down_in, wd_ref[cols, :])
            gate = gates[rows, cols].astype(F32)
            up = ups[rows, cols].astype(F32)
            sig = jax.nn.sigmoid(gate)
            gate_back = (back * up * sig * (1.0 + gate * (1.0 - sig))).astype(BF16)
            up_back = (back * gate * sig).astype(BF16)
            gates[rows, cols] = gate_back
            ups[rows, cols] = up_back
            total += dot_nt(gate_back, wide_weights[0][:, cols]) + dot_nt(up_back, wide_weights[1][:, cols])
        for i in range(2):
            offer(2, 2 * j + i, 1, 2 * j + i, total[i * LEN:(i + 1) * LEN])

    def attention_back(m):
        rows = rows_of(m, 1)
        back = exchanged(2, m, 1, m)
        mid = middle[rows, :]
        factor = rms_factor(mid)
        gain_acc[0:1, :] += jnp.sum(back * mid * factor, axis=0, keepdims=True)
        mid_back = gin[rows, :].astype(F32) + norm_back(mid, factor, back * gf_ref[...])
        middle_back[rows, :] = mid_back
        mixed_back = dot_nt(mid_back.astype(BF16), wo_ref[...]).astype(BF16)
        cosine, sine = cos_ref[:, :HEAD], sin_ref[:, :HEAD]
        query, key, value = qs[rows, :], ks[rows, :], vs[rows, :]
        query_turn = turned(query).astype(BF16)
        key_turn = turned(key).astype(BF16)
        query_out, key_out, value_out = [], [], []
        for g in range(GROUPS):
            cols = slice(g * HEAD, (g + 1) * HEAD)
            prob = probs[m, g]
            prob_f = prob.astype(F32)
            out_back = stacked(mixed_back, g)
            value_out.append(dot_tn(prob, out_back).astype(BF16))
            prob_back = dot_nt(out_back, value[:, cols])
            score_back = (
                prob_f * (prob_back - jnp.sum(prob_back * prob_f, axis=-1, keepdims=True))
            ).astype(BF16)
            both = jnp.concatenate([key[:, cols], key_turn[:, cols]], axis=1)
            both_back = dot(score_back, both) * HEAD**-0.5
            for t in range(3):
                one = both_back[t * LEN:(t + 1) * LEN]
                query_out.append((one[:, :HEAD] * cosine - one[:, HEAD:] * sine).astype(BF16))
            both = jnp.concatenate([stacked(query, g), stacked(query_turn, g)], axis=1)
            one = dot_tn(score_back, both) * HEAD**-0.5
            key_out.append((one[:, :HEAD] * cosine - one[:, HEAD:] * sine).astype(BF16))
        qkv_back[rows, :QW + 2 * KW] = jnp.concatenate(query_out + key_out + value_out, axis=1)
        offer(
            3, m, 1, m,
            dot(qkv_back[rows, :QW], wq_ref[...])
            + dot(qkv_back[rows, QW:QW + KW], wk_ref[...])
            + dot(qkv_back[rows, QW + KW:QW + 2 * KW], wv_ref[...]),
        )

    def finish_back(m):
        rows = rows_of(m, 1)
        back = exchanged(3, m, 1, m)
        h = hin[rows, :].astype(F32)
        factor = rms_factor(h)
        gain_acc[1:2, :] += jnp.sum(back * h * factor, axis=0, keepdims=True)
        snd_a[rows, :] = (
            middle_back[rows, :] + norm_back(h, factor, back * ga_ref[...])
        ).astype(BF16)

        @pl.when(section == 1)
        def _():
            pass_on(1, m, 1, m).start()

        start_emit(1, m)

    def flush(out, slot, half, col, wide):
        return pltpu.make_async_copy(
            g_stage.at[slot, :, :, :, pl.ds(0, wide)],
            out.at[pl.ds(2 * half, 2), :, :, pl.ds(col, wide)],
            g_sem.at[slot],
        )

    def product(right, right_col, out, col, count):
        def step(k, carry):
            slot, half = lax.rem(k, G_SLOTS), lax.rem(k, 2)

            @pl.when(k >= G_SLOTS)
            def _():
                flush(out, slot, half, 0, 512).wait()

            start = pl.multiple_of(lax.div(k, 2) * 512, 512)
            left = xt[pl.ds(pl.multiple_of(half * 640, 640), 640), :]
            g_stage[slot] = (
                dot(left, right[:, pl.ds(right_col + start, 512)])
                .astype(BF16)
                .reshape(2, RING, PIECE, 512)
            )
            flush(out, slot, half, pl.multiple_of(col + start, 128), 512).start()
            return carry

        lax.fori_loop(0, 2 * count, step, 0)
        for k in range(max(0, 2 * count - G_SLOTS), 2 * count):
            flush(out, k % G_SLOTS, k % 2, 0, 512).wait()

    def features(source):
        for c in range(0, TOKENS, 256):
            block = slice(c, c + 256)
            xt[:, block] = dot_nt(place_ref[...], source[block, :].astype(BF16)).astype(BF16)

    def down_gradient(_):
        features(gin)
        product(hidden, 0, g0, 0, 3)
        ring.run("a0", "a1")

    def gate_gradient(_):
        features(ffn_in)
        product(gates, 0, g1, 0, 3)
        ring.run("a2", "a3", "b00", "b01")
        product(ups, 0, g2, 0, 3)
        ring.run("a4", "a5")

    def out_gradient():
        features(middle_back)
        product(mixed, 0, g3, 0, 1)
        gains = jnp.concatenate(
            [jnp.zeros((64, WIDTH), F32), gain_acc[...], jnp.zeros((56, WIDTH), F32)], axis=0
        ).astype(BF16)
        last = (dot(xt[...], mixed[:, 512:640]) + dot_nt(place_ref[...], gains)).astype(BF16)
        for half in range(2):
            g_stage[half, :, :, :, 0:128] = last[half * 640:half * 640 + 640].reshape(
                2, RING, PIECE, 128
            )
            flush(g3, half, half, 512, 128).start()
        for half in range(2):
            flush(g3, half, half, 512, 128).wait()

    def plan(t, ours, theirs):
        index = jnp.int32(-1)
        for k, (one, other) in enumerate(zip(ours, theirs)):
            if one >= 0 or other >= 0:
                index = jnp.where(t == k, jnp.where(section == 0, one, other), index)
        return index

    def tick(t, carry):
        def do(work, ours, theirs):
            index = plan(t, ours, theirs)

            @pl.when(index >= 0)
            def _():
                work(index)

        def finish_forward(m):
            finish(m, 1, m)
            pass_on(0, m, 1, m).start()
            start_emit(0, m)

        @pl.when(t == 1)
        def _():
            for copy in loads[7:] + wide_loads:
                copy.wait()

        do(
            attention,
            (0, 1, 2, -1, 3, -1, -1, -1, -1, -1, -1, -1, -1, -1),
            (0, 1, 2, -1, -1, 3, -1, -1, -1, -1, -1, -1, -1, -1),
        )
        do(
            finish_forward,
            (-1, -1, -1, -1, 0, 1, 2, 3, -1, -1, -1, -1, -1, -1),
            (-1, -1, -1, -1, -1, -1, -1, -1, -1, -1, -1, -1, -1, -1),
        )
        do(
            feed_forward,
            (-1, -1, 0, 1, 2, 3, -1, -1, -1, -1, -1, -1, -1, -1),
            (-1, -1, 0, 1, 2, -1, -1, 3, -1, -1, -1, -1, -1, -1),
        )

        @pl.when((t == 7) & (section == 0))
        def _():
            for m in range(SEQS):
                pass_on(0, m, 1, m).wait_send()
                settle_emit(0, m)

        do(
            finish_back,
            (-1, -1, -1, -1, -1, -1, -1, -1, -1, -1, -1, 0, 1, 2),
            (-1, -1, -1, -1, -1, -1, -1, 0, 1, -1, -1, 2, 3, -1),
        )
        do(
            feed_forward_back,
            (-1, -1, -1, -1, -1, -1, -1, 0, -1, 1, -1, -1, -1, -1),
            (-1, -1, -1, 0, -1, -1, -1, 1, -1, -1, -1, -1, -1, -1),
        )
        do(
            down_gradient,
            (-1, -1, -1, -1, -1, -1, -1, -1, -1, 0, -1, -1, -1, -1),
            (-1, -1, -1, -1, -1, -1, -1, -1, 0, -1, -1, -1, -1, -1),
        )
        do(
            gate_gradient,
            (-1, -1, -1, -1, -1, -1, -1, -1, -1, 0, -1, -1, -1, -1),
            (-1, -1, -1, -1, -1, -1, -1, -1, -1, -1, 0, -1, -1, -1),
        )
        do(
            attention_back,
            (-1, -1, -1, -1, -1, -1, -1, 0, 1, 2, 3, -1, -1, -1),
            (-1, -1, -1, -1, -1, 0, 1, -1, 2, 3, -1, -1, -1, -1),
        )
        return carry

    wide_loads = []

    def first_phase(wg_ref, wu_ref):
        wide_weights[:] = [wg_ref, wu_ref]
        wide_loads[:] = [
            pltpu.make_async_copy(wg_in, wg_ref, load_sem.at[9]),
            pltpu.make_async_copy(wu_in, wu_ref, load_sem.at[10]),
        ]
        for copy in wide_loads:
            copy.start()
        for copy in loads[:7]:
            copy.wait()
        lax.fori_loop(0, 14, tick, 0)

    pl.run_scoped(first_phase, pltpu.VMEM((WIDTH, FF), BF16), pltpu.VMEM((WIDTH, FF), BF16))

    def second_phase(hs, ls, rs):
        steps = make_ring(hs, ls, rs)
        steps.run("b0", "b1")

        @pl.when(section == 0)
        def _():
            finish_back(3)

        @pl.when(section == 1)
        def _():
            for j in range(2):
                offer(1, 2 * j, 2, j, dot(hidden[rows_of(2 * j, 2), :], wd_ref[...]))

        steps.run("b02", "b03")
        out_gradient()
        steps.run("a6", "b2", "b3", "b04", "b05")
        features(normed)
        product(qkv_back, 0, g3, 640, 1)
        steps.run("a7")
        product(qkv_back, 512, g3, 1152, 1)
        steps.run(
            "a8", "a9", "c00", "c01", "c02", "c03", "b4", "b5", "b06", "b07", "b08", "b09",
            "c0", "c1", "c2", "c3", "b6", "b7", "b8", "b9", "d0", "d1", "c04", "c4",
            "d2", "d3", "e0", "e1", "c05", "c06", "c5", "c6", "e2", "e3", "f0", "f1",
        )

        @pl.when(section == 1)
        def _():
            for j in range(2):
                finish(2 * j, 2, j)
                start_emit(0, 2 * j)
                start_emit(0, 2 * j + 1)

        steps.run(
            "c07", "c08", "c7", "c8", "d4", "d5", "e4", "c09", "d6", "e5", "c9", "d7",
            "d8", "f2", "f3", "d9", "e6", "e7", "e8", "e9", "f4", "f5", "f6", "f7",
            "f8", "f9",
        )
        steps.finish()

    pl.run_scoped(
        second_phase,
        *[
            pltpu.VMEM((slots, RING, PIECE, WIDE), BF16)
            for slots in (H_SLOTS, L_SLOTS, L_SLOTS)
        ],
    )

    for m in range(SEQS):
        for s in range(2):
            @pl.when((section == s) & (shard == 1))
            def _():
                fetch(s, m)[1]().wait_send()

        @pl.when(section == 1)
        def _():
            settle_emit(0, m)

        settle_emit(1, m)

        @pl.when(shard == 1)
        def _():
            for which in range(2):
                emit(which, m)[1]().wait_recv()

    for j in range(SEQS):
        @pl.when(section == 1)
        def _():
            pass_on(1, j, 1, j).wait_send()


def deliver_kernel(
    act_in, ig_in, down, gate, up, mix,
    act, ig, gain_a, query, key, value, out, gain_f, gate_out, up_out, down_out,
):
    act[...] = act_in[...]
    ig[...] = ig_in[...]
    for target, source, first, wide in (
        (query, mix, 640, QW),
        (key, mix, 640 + QW, KW),
        (value, mix, 640 + QW + KW, KW),
        (out, mix, 0, QW),
        (gate_out, gate, 0, FF),
        (up_out, up, 0, FF),
        (down_out, down, 0, FF),
    ):
        target[...] = source[0:OWN, first:first + wide].reshape(OWN, 1, wide)
    gains = mix[:, 512:640].T
    gain_f[...] = gains[64:65, 0:OWN]
    gain_a[...] = gains[65:66, 0:OWN]


def on_device(x, cot, ga, wq, wk, wv, wo, gf, wg, wu, wd):
    cosine, sine = rope_tables()
    vmem = pl.BlockSpec(memory_space=pltpu.VMEM)
    any_ = pl.BlockSpec(memory_space=pl.ANY)
    sds = jax.ShapeDtypeStruct
    rows = (TOKENS, WIDTH)
    dma = pltpu.SemaphoreType.DMA
    operands = (
        wq[0].T, wk[0].T, wv[0].T, wo[0], jnp.asarray(cosine), jnp.asarray(sine),
        jnp.asarray(turn_matrix(), BF16), wg[0], wu[0], wd[0], jnp.asarray(place_matrix(), BF16),
    )

    def buffer(shape, kind=BF16):
        return pltpu.VMEM(shape, kind)

    scratch = [
        buffer(item.shape, item.dtype) for k, item in enumerate(operands) if k not in (7, 8)
    ]
    scratch += [buffer(rows)] * 3
    scratch += [
        buffer((TOKENS, QW)),
        buffer((TOKENS, KW)),
        buffer((TOKENS, KW)),
        buffer((SEQS, GROUPS, 3 * LEN, LEN)),
        buffer((TOKENS, 640)),
        buffer(rows, F32),
        buffer(rows),
        buffer((TOKENS, FF)),
        buffer((TOKENS, FF)),
        buffer((TOKENS, FF)),
        buffer((TOKENS, 1024)),
        buffer((8, WIDTH), F32),
        buffer((ROWS, TOKENS)),
        buffer(rows, F32),
    ]
    scratch += [buffer(rows)] * 4
    scratch += [
        buffer((G_SLOTS, 2, RING, PIECE, 512)),
        buffer((C_SLOTS, RING, PIECE, WIDE)),
    ]
    for _, _, wide, cut, _ in BLOCKS:
        scratch += [buffer((RING, PIECE, cut)), buffer((RING, PIECE, wide - cut))]
    for _, _, wide, cut, _ in BLOCKS:
        scratch += [
            buffer((PIECE, cut)),
            buffer((PIECE, wide - cut)),
            buffer((PIECE, wide)),
            buffer((PIECE, wide)),
            buffer((PIECE + 48, wide)),
        ]
    scratch += [
        dma((len(operands),)),
        dma((2, SEQS)),
        dma((2, SEQS)),
        dma((4, SEQS)),
        dma((4, SEQS)),
        dma((2, SEQS)),
        dma((2, SEQS)),
        dma((2, SEQS)),
        dma((2, SEQS)),
        dma((G_SLOTS,)),
        dma((COUNT, 13)),
        dma((COUNT, 13)),
        dma((COUNT, 5)),
    ]
    outs = pl.pallas_call(
        layer_kernel,
        out_shape=(
            [sds(x.shape, BF16)] * 2
            + [sds((RING, RING, PIECE, columns), BF16) for columns in PARTS]
            + [sds((RING, PIECE, COLUMNS), BF16)] * 2
            + [sds((40, columns), F32) for columns in PARTS]
        ),
        in_specs=[any_] * 2 + [vmem] * 2 + [any_] * len(operands),
        out_specs=[any_] * 8 + [vmem] * 4,
        scratch_shapes=scratch,
        compiler_params=pltpu.CompilerParams(
            collective_id=0, has_side_effects=True, vmem_limit_bytes=63 * 2**20
        ),
        cost_estimate=pl.CostEstimate(
            flops=26 * 10**9, bytes_accessed=60 * 10**6, transcendentals=10**7
        ),
        name="layer",
    )(x, cot, ga, gf, *operands)
    acts, grads = outs[:2]
    done = pl.pallas_call(
        deliver_kernel,
        out_shape=(
            [sds(x.shape, BF16)] * 2
            + [sds((1, OWN), F32)]
            + [sds((OWN, 1, wide), F32) for wide in (QW, KW, KW, QW)]
            + [sds((1, OWN), F32)]
            + [sds((OWN, 1, FF), F32)] * 3
        ),
        in_specs=[vmem] * 6,
        out_specs=[vmem] * 11,
        name="deliver",
    )(acts, grads, *outs[8:])
    act, ig, gain_a, query, key, value, out, gain_f, gate, up, down = done

    def rows_out(item):
        return item.transpose(1, 0, 2)

    def columns_out(item):
        return item.transpose(1, 2, 0)

    return (
        act[None], ig[None], gain_a, rows_out(query), rows_out(key), rows_out(value),
        columns_out(out), gain_f, rows_out(gate), rows_out(up), columns_out(down),
    )


def solution(mesh):
    in_specs = (
        P("replica", None, None),
        P("replica", None, None),
        P("section", None),
        P("section", None, "shard"),
        P("section", None, "shard"),
        P("section", None, "shard"),
        P("section", "shard", None),
        P("section", None),
        P("section", None, "shard"),
        P("section", None, "shard"),
        P("section", "shard", None),
    )
    out_specs = (
        P("section", "replica", None, None),
        P("section", "replica", None, None),
        P("section", "replica"),
        P("section", "replica", "shard"),
        P("section", "replica", "shard"),
        P("section", "replica", "shard"),
        P("section", "shard", "replica"),
        P("section", "replica"),
        P("section", "replica", "shard"),
        P("section", "replica", "shard"),
        P("section", "shard", "replica"),
    )
    return jax.shard_map(
        on_device, mesh=mesh, in_specs=in_specs, out_specs=out_specs, check_vma=False
    )
```

time: 321 us -> 211 us (0.66)
  Pallas kernels: 301 us -> 210 us
  local copies, waits for them, and re-layouts: 18 us -> 0 us
    pallas_call x2, Pallas kernels: 301 us -> 210 us  [the longest x1 206 us: on_device(): pl.pallas_call(layer_kernel, out_shape=[sds(x.shape, BF16)] * 2 + [sds((R...]
    unnamed x22 -> x0, local copies, waits for them, and re-layouts: 13.4 us -> none
where the time goes in v2:
time: 211 us
  Pallas kernels  210 us (100%)
    pallas_call x1, Pallas kernels, on_device(): pl.pallas_call(layer_kernel, out_shape=[sds(x.shape, BF16)] * 2 + [sds((R...  206 us

profile of v2, /device:TPU:0, one launch (start us, length us, event | category | flops | bytes accessed | tf_op | source)
XLA Modules:
  0.0 210.7 jit_solution(16854221849840797877)
XLA Ops:
  0.6 206.3 %layer.1 = (bf16[4,128,1152]{2,1,0:T(8,128)(2,1)}, bf16[4,128,1152]{2,1,0:T(8,128)(2,1)}, bf16[4,4,80,1536]{3,2,1,0:T(8,128)(2,1)}, bf16[4,4,80,1536]{3,2,1,0:T(...) custom-call(bf16[4,128,1152]{2,1,0:T(8,128)(2,1)} %x_ref.1, ...), custom_call_target="tpu_custom_call" | custom-call | flops 25999998976 | bytes 60000000 | tf_op jit(solution)/shard_map/layer/pallas_call | solution.py:953
  207.0 3.7 %deliver.1 = (bf16[4,128,1152]{2,1,0:T(8,128)(2,1)}, bf16[4,128,1152]{2,1,0:T(8,128)(2,1)}, f32[1,36]{1,0:T(1,128)}, f32[36,1,576]{2,1,0:T(1,128)}, f32[36,1,192...) custom-call(bf16[4,128,1152]{2,1,0:T(8,128)(2,1)} %get-tuple-element, ...), custom_call_target="tpu_custom_call" | custom-call | tf_op jit(solution)/shard_map/deliver/pallas_call | solution.py:973

commit v3 on v2

--- a/solution.py
+++ b/solution.py
@@ -752,7 +752,7 @@
 
         do(
             finish_back,
-            (-1, -1, -1, -1, -1, -1, -1, -1, -1, -1, -1, 0, 1, 2),
+            (-1,) * 14,
             (-1, -1, -1, -1, -1, -1, -1, 0, 1, -1, -1, 2, 3, -1),
         )
         do(
@@ -797,24 +797,29 @@
         steps = make_ring(hs, ls, rs)
         steps.run("b0", "b1")
 
-        @pl.when(section == 0)
-        def _():
-            finish_back(3)
-
         @pl.when(section == 1)
         def _():
             for j in range(2):
                 offer(1, 2 * j, 2, j, dot(hidden[rows_of(2 * j, 2), :], wd_ref[...]))
 
         steps.run("b02", "b03")
-        out_gradient()
-        steps.run("a6", "b2", "b3", "b04", "b05")
         features(normed)
         product(qkv_back, 0, g3, 640, 1)
-        steps.run("a7")
+        steps.run("a7", "b2", "b3", "b04", "b05")
         product(qkv_back, 512, g3, 1152, 1)
+        steps.run("a8", "a9")
+
+        @pl.when(section == 0)
+        def _():
+            def late_finish(m, carry):
+                finish_back(m)
+                return carry
+
+            lax.fori_loop(0, SEQS, late_finish, 0)
+
+        out_gradient()
         steps.run(
-            "a8", "a9", "c00", "c01", "c02", "c03", "b4", "b5", "b06", "b07", "b08", "b09",
+            "a6", "c00", "c01", "c02", "c03", "b4", "b5", "b06", "b07", "b08", "b09",
             "c0", "c1", "c2", "c3", "b6", "b7", "b8", "b9", "d0", "d1", "c04", "c4",
             "d2", "d3", "e0", "e1", "c05", "c06", "c5", "c6", "e2", "e3", "f0", "f1",
         )

time: 211 us -> 209 us (level)
    pallas_call x1, Pallas kernels: 206 us -> 204 us  [on_device(): pl.pallas_call(layer_kernel, out_shape=[sds(x.shape, BF16)] * 2 + [sds((R...]
where the time goes in v3:
time: 209 us; the launch traced here: 208 us
  Pallas kernels  208 us (100%)
    pallas_call x1, Pallas kernels, on_device(): pl.pallas_call(layer_kernel, out_shape=[sds(x.shape, BF16)] * 2 + [sds((R...  204 us

profile of v3, /device:TPU:0, one launch (start us, length us, event | category | flops | bytes accessed | tf_op | source)
XLA Modules:
  0.0 208.2 jit_solution(12132991416469213663)
XLA Ops:
  0.6 203.9 %layer.1 = (bf16[4,128,1152]{2,1,0:T(8,128)(2,1)}, bf16[4,128,1152]{2,1,0:T(8,128)(2,1)}, bf16[4,4,80,1536]{3,2,1,0:T(8,128)(2,1)}, bf16[4,4,80,1536]{3,2,1,0:T(...) custom-call(bf16[4,128,1152]{2,1,0:T(8,128)(2,1)} %x_ref.1, ...), custom_call_target="tpu_custom_call" | custom-call | flops 25999998976 | bytes 60000000 | tf_op jit(solution)/shard_map/layer/pallas_call | solution.py:958
  204.5 3.7 %deliver.1 = (bf16[4,128,1152]{2,1,0:T(8,128)(2,1)}, bf16[4,128,1152]{2,1,0:T(8,128)(2,1)}, f32[1,36]{1,0:T(1,128)}, f32[36,1,576]{2,1,0:T(1,128)}, f32[36,1,192...) custom-call(bf16[4,128,1152]{2,1,0:T(8,128)(2,1)} %get-tuple-element, ...), custom_call_target="tpu_custom_call" | custom-call | tf_op jit(solution)/shard_map/deliver/pallas_call | solution.py:978
